TPU v7x, 512 devices: a whole 4x4x16 slice. The times are simulated.
512 devices in a mesh: ctx: 128 (over y_hi, z, x), tp: 4 (over y_lo, core).
Axes of the slice: x: 4, y: 4 (y_hi: 2, y_lo: 2; y = y_hi * 2 + y_lo), z: 16, core: 2. Of those that a mesh axis runs over, the one named last changes fastest.
Arguments:
- gate_query: bfloat16 [16384, 1024], P('ctx', 'tp'), may hold values from -24 to 24, as said below
- key_proj: bfloat16 [16384, 1024], P('ctx', 'tp'), may hold values from -6 to 6
- value_proj: bfloat16 [16384, 1024], P('ctx', 'tp'), may hold values from -6 to 6
- long_filter: float32 [16384, 1024], P('ctx', 'tp'), may hold values from -6 to 6
- out_gain: float32 [1024], P('tp'), may hold values from 0.1 to 1.9
- cotangent: bfloat16 [16384, 1024], P('ctx', 'tp'), may hold values from -24 to 24, as said below
Outputs:
- output: bfloat16 [16384, 1024], P('ctx', 'tp')
- grad_query: bfloat16 [16384, 1024], P('ctx', 'tp')
- grad_key: bfloat16 [16384, 1024], P('ctx', 'tp')
- grad_value: bfloat16 [16384, 1024], P('ctx', 'tp')
- grad_filter: float32 [16384, 1024], P('ctx', 'tp')
- grad_gain: float32 [1024], P('tp')
Inputs may be any that keep to these rules, and one draw needn't show every extreme that they name: `gate_query`: real values. `cotangent`: real values.
All inputs are finite; a program needn't handle non-finite values.
Results may differ from a plain program's by a relative error of at most 0.0019.
Values sent between devices are 32-bit elements; how exact they have to be, the bound alone decides.
No kernel may reach another device: no remote copies, remote signals or barrier semaphores. Data moves between devices by JAX's collectives and lax.ppermute only.
A program may use at most 64 MiB of HBM per device.

v0:
```python
import math

import jax
import jax.numpy as jnp
from jax import lax
from jax.sharding import PartitionSpec as P

norm_eps = 1e-06


def phase_table(first_idx, second_idx, period, sign):
    phase = first_idx * second_idx % period
    angle = sign * 2.0 * math.pi / period * phase.astype(jnp.float32)
    return (jnp.cos(angle), jnp.sin(angle))


def iota_of(count):
    return jnp.arange(count, dtype=jnp.int32)


def mix_sum(form, table, operand):
    return jnp.einsum(form, table, operand, precision=lax.Precision.HIGHEST)


def local_dft(real_in, imag_in, axis, sign):
    total = real_in.shape[axis]
    factor_one = 1
    for divisor in range(1, math.isqrt(total) + 1):
        if total % divisor == 0:
            factor_one = divisor
    factor_two = total // factor_one
    real_mv = jnp.moveaxis(real_in, axis, -1)
    imag_mv = jnp.moveaxis(imag_in, axis, -1)
    leading = real_mv.shape[:-1]
    real_mv = real_mv.reshape(leading + (factor_one, factor_two))
    imag_mv = imag_mv.reshape(leading + (factor_one, factor_two))
    cos_p, sin_p = phase_table(
        iota_of(factor_one)[:, None], iota_of(factor_one)[None, :], factor_one, sign
    )
    real_one = mix_sum("ma,...ab->...mb", cos_p, real_mv) - mix_sum(
        "ma,...ab->...mb", sin_p, imag_mv
    )
    imag_one = mix_sum("ma,...ab->...mb", cos_p, imag_mv) + mix_sum(
        "ma,...ab->...mb", sin_p, real_mv
    )
    cos_t, sin_t = phase_table(
        iota_of(factor_one)[:, None], iota_of(factor_two)[None, :], total, sign
    )
    real_tw = real_one * cos_t - imag_one * sin_t
    imag_tw = real_one * sin_t + imag_one * cos_t
    cos_q, sin_q = phase_table(
        iota_of(factor_two)[:, None], iota_of(factor_two)[None, :], factor_two, sign
    )
    real_two = mix_sum("nb,...mb->...nm", cos_q, real_tw) - mix_sum(
        "nb,...mb->...nm", sin_q, imag_tw
    )
    imag_two = mix_sum("nb,...mb->...nm", cos_q, imag_tw) + mix_sum(
        "nb,...mb->...nm", sin_q, real_tw
    )
    real_two = jnp.moveaxis(real_two.reshape(leading + (total,)), -1, axis)
    imag_two = jnp.moveaxis(imag_two.reshape(leading + (total,)), -1, axis)
    return (real_two, imag_two)


def seq_forward(signals):
    n_ctx = lax.axis_size("ctx")
    my_index = lax.axis_index("ctx")
    count, seg_rows, seg_chans = signals.shape
    slice_len = seg_rows // n_ctx
    coarse = 2 * n_ctx
    period = coarse * seg_rows
    pieces = lax.all_to_all(
        signals.reshape(count, 1, seg_rows, seg_chans),
        "ctx",
        split_axis=2,
        concat_axis=1,
        tiled=True,
    )
    cos_a, sin_a = phase_table(iota_of(coarse)[:, None], iota_of(n_ctx)[None, :], coarse, -1.0)
    real_part = mix_sum("ka,sabc->skbc", cos_a, pieces)
    imag_part = mix_sum("ka,sabc->skbc", sin_a, pieces)
    col_index = my_index * slice_len + iota_of(slice_len)
    cos_t, sin_t = phase_table(iota_of(coarse)[:, None], col_index[None, :], period, -1.0)
    cos_t = cos_t[:, :, None]
    sin_t = sin_t[:, :, None]
    twisted = jnp.stack(
        [real_part * cos_t - imag_part * sin_t, real_part * sin_t + imag_part * cos_t], 1
    )
    moved = lax.all_to_all(twisted, "ctx", split_axis=2, concat_axis=3, tiled=True)
    real_out, imag_out = local_dft(moved[:, 0], moved[:, 1], 2, -1.0)
    spectra = jnp.stack([real_out, imag_out], 1)
    spectra = lax.all_to_all(spectra, "ctx", split_axis=3, concat_axis=2, tiled=True)
    return spectra


def seq_inverse(spectra):
    n_ctx = lax.axis_size("ctx")
    my_index = lax.axis_index("ctx")
    spectra = lax.all_to_all(spectra, "ctx", split_axis=2, concat_axis=3, tiled=True)
    count = spectra.shape[0]
    seg_rows = spectra.shape[3]
    seg_chans = spectra.shape[4]
    coarse = 2 * n_ctx
    period = coarse * seg_rows
    real_part, imag_part = local_dft(spectra[:, 0], spectra[:, 1], 2, 1.0)
    freq_index = 2 * my_index + iota_of(2)
    cos_t, sin_t = phase_table(freq_index[:, None], iota_of(seg_rows)[None, :], period, 1.0)
    cos_t = cos_t[:, :, None]
    sin_t = sin_t[:, :, None]
    twisted = jnp.stack(
        [real_part * cos_t - imag_part * sin_t, real_part * sin_t + imag_part * cos_t], 1
    )
    moved = lax.all_to_all(twisted, "ctx", split_axis=3, concat_axis=2, tiled=True)
    cos_a, sin_a = phase_table(iota_of(n_ctx)[:, None], iota_of(coarse)[None, :], coarse, 1.0)
    result = mix_sum("ak,skbc->sabc", cos_a, moved[:, 0]) - mix_sum(
        "ak,skbc->sabc", sin_a, moved[:, 1]
    )
    result = result * (1.0 / period)
    back = lax.all_to_all(result, "ctx", split_axis=1, concat_axis=2, tiled=True)
    return back.reshape(count, seg_rows, seg_chans)


def forward_all(signals):
    return seq_forward(signals)


def inverse_all(spectra):
    return seq_inverse(spectra)


def spec_product(left_spec, right_spec, conjugate):
    left_real = left_spec[0]
    left_imag = -left_spec[1] if conjugate else left_spec[1]
    return jnp.stack(
        [
            left_real * right_spec[0] - left_imag * right_spec[1],
            left_real * right_spec[1] + left_imag * right_spec[0],
        ]
    )


def per_device(gate_query, key_proj, value_proj, long_filter, out_gain, cotangent):
    seg_rows, seg_chans = gate_query.shape
    length = seg_rows * lax.axis_size("ctx")
    channels = seg_chans * lax.axis_size("tp")
    filt_scale = 1.0 / math.sqrt(length)
    query_f = gate_query.astype(jnp.float32)
    key_f = key_proj.astype(jnp.float32)
    value_f = value_proj.astype(jnp.float32)
    cot_f = cotangent.astype(jnp.float32)
    mixed_in = key_f * value_f
    filt_in = long_filter * filt_scale
    spectra = forward_all(jnp.stack([filt_in, mixed_in]))
    filt_spec = spectra[0]
    mixed_spec = spectra[1]
    conv_out = inverse_all(spec_product(filt_spec, mixed_spec, False)[None])[0]
    gated_out = query_f * conv_out
    sum_sq = lax.psum(jnp.sum(gated_out * gated_out, axis=1), "tp")
    inv_rms = lax.rsqrt(sum_sq / channels + norm_eps)[:, None]
    output = (gated_out * inv_rms * out_gain).astype(jnp.bfloat16)
    scaled = cot_f * out_gain
    row_dot = lax.psum(jnp.sum(scaled * gated_out, axis=1), "tp")[:, None] / channels
    grad_gain = lax.psum(jnp.sum(cot_f * gated_out * inv_rms, axis=0), "ctx")
    d_gated = inv_rms * scaled - gated_out * inv_rms * inv_rms * inv_rms * row_dot
    grad_query = (d_gated * conv_out).astype(jnp.bfloat16)
    d_conv = d_gated * query_f
    conv_spec = forward_all(d_conv[None])[0]
    results = inverse_all(
        jnp.stack(
            [spec_product(filt_spec, conv_spec, True), spec_product(mixed_spec, conv_spec, True)]
        )
    )
    d_mixed = results[0]
    grad_key = (d_mixed * value_f).astype(jnp.bfloat16)
    grad_value = (d_mixed * key_f).astype(jnp.bfloat16)
    grad_filter = results[1] * filt_scale
    return (output, grad_query, grad_key, grad_value, grad_filter, grad_gain)


def solution(mesh):
    return jax.shard_map(
        per_device,
        mesh=mesh,
        in_specs=(
            P("ctx", "tp"),
            P("ctx", "tp"),
            P("ctx", "tp"),
            P("ctx", "tp"),
            P("tp"),
            P("ctx", "tp"),
        ),
        out_specs=(
            P("ctx", "tp"),
            P("ctx", "tp"),
            P("ctx", "tp"),
            P("ctx", "tp"),
            P("ctx", "tp"),
            P("tp"),
        ),
        check_vma=False,
    )
```

profile of v0, /device:TPU:24, one launch (start us, length us, event | category | flops | bytes accessed | tf_op | source)
XLA Modules:
  0.0 946.1 jit_solution(17653512178466433651)
XLA Ops:
  0.6 0.9 broadcast_multiply_fusion
  2.5 0.9 maximum_bitcast_fusion.3
  3.5 22.2 %all-to-all-start = ((f32[2,1,128,256]{3,0,1,2:T(2,128)}), f32[2,1,128,256]{3,0,1,2:T(2,128)S(1)}, u32[]{:S(2)}, u32[]{:S(2)}) async-start(f32[2,1,128,256]{3,0,1,2:T(2,128)} %maximum_bitcast_fusion.3), calls=%async_computation | async-start | bytes 524288 | tf_op jit(solution)/shard_map/all_to_all | solution.py:72
  25.7 22.4 %all-to-all-done = f32[2,1,128,256]{3,0,1,2:T(2,128)S(1)} async-done(((f32[2,1,128,256]{3,0,1,2:T(2,128)}), f32[2,1,128,256]{3,0,1,2:T(2,128)S(1)}, u32[]{:S(2)}, u32[]{:S(2)}) %all-to-all-start) | async-done | bytes 262176 | tf_op jit(solution)/shard_map/all_to_all | solution.py:72
  48.2 1.1 convolution_bitcast_fusion
  49.3 1.1 subtract_bitcast_fusion
  50.5 1.3 copy.171
  51.8 9.5 %all-to-all-start.1 = ((f32[2,2,256,1,256]{4,0,3,1,2:T(2,128)}), f32[2,2,256,1,256]{4,0,3,1,2:T(2,128)S(1)}, u32[]{:S(2)}, u32[]{:S(2)}) async-start(f32[2,2,256,1,256]{4,0,3,1,2:T(2,128)} %copy.171), calls=%async_computation.1 | async-start | bytes 2097152 | tf_op jit(solution)/shard_map/all_to_all | solution.py:89
  61.4 54.4 %all-to-all-done.1 = f32[2,2,256,1,256]{4,0,3,1,2:T(2,128)S(1)} async-done(((f32[2,2,256,1,256]{4,0,3,1,2:T(2,128)}), f32[2,2,256,1,256]{4,0,3,1,2:T(2,128)S(1)}, u32[]{:S(2)}, u32[]{:S(2)}) %all-to-all-start.1) | async-done | bytes 1048608 | tf_op jit(solution)/shard_map/all_to_all | solution.py:89
  116.3 0.8 fusion.412
  117.5 0.9 fusion.49
  118.7 0.9 fusion.45
  119.6 0.9 fusion.7
  120.4 1.0 multiply_subtract_fusion.1
  125.1 0.8 copy.185
  125.9 62.4 %all_to_all.174 = f32[2,2,2,128,256]{4,2,0,1,3:T(2,128)S(1)} all-to-all(f32[2,2,2,128,256]{4,2,0,1,3:T(2,128)S(1)} %copy.185), channel_id=1, replica_groups=mesh['ctx'=128,'tp'=4] {'ctx'}, dimensions={3} | all-to-all | bytes 2097152 | tf_op jit(solution)/shard_map/all_to_all | solution.py:92
  190.8 1.2 copy.186
  191.9 9.0 all-to-all-start.3
  201.1 30.2 %all-to-all-done.3 = f32[1,2,256,1,256]{4,3,1,0,2:T(1,128)S(1)} async-done(((f32[1,2,256,1,256]{4,3,1,0,2:T(1,128)}), f32[1,2,256,1,256]{4,3,1,0,2:T(1,128)S(1)}, u32[]{:S(2)}, u32[]{:S(2)}) %all-to-all-start.3) | async-done | bytes 524320 | tf_op jit(solution)/shard_map/all_to_all | solution.py:99
  237.1 40.5 %all_to_all.175 = f32[1,2,2,128,256]{4,2,1,0,3:T(2,128)S(1)} all-to-all(f32[1,2,2,128,256]{4,2,1,0,3:T(2,128)S(1)} %copy.199), channel_id=1, replica_groups=mesh['ctx'=128,'tp'=4] {'ctx'}, dimensions={3} | all-to-all | bytes 1048576 | tf_op jit(solution)/shard_map/all_to_all | solution.py:113
  278.2 1.0 fusion.53
  279.2 1.0 fusion.19
  280.3 24.5 %all_to_all.176 = f32[1,128,1,256]{3,2,0,1:T(1,128)S(1)} all-to-all(f32[1,128,1,256]{3,2,0,1:T(1,128)S(1)} %copy.201), channel_id=1, replica_groups=mesh['ctx'=128,'tp'=4] {'ctx'}, dimensions={1} | all-to-all | bytes 262144 | tf_op jit(solution)/shard_map/all_to_all | solution.py:119
  305.0 5.7 psum.21
  311.5 6.1 psum.22
  317.6 0.8 fusion.90
  318.5 25.2 %all_to_all.177 = f32[1,1,128,256]{3,1,0,2:T(1,128)S(1)} all-to-all(f32[1,1,128,256]{3,1,0,2:T(1,128)S(1)} %copy.202), channel_id=1, replica_groups=mesh['ctx'=128,'tp'=4] {'ctx'}, dimensions={2} | all-to-all | bytes 262144 | tf_op jit(solution)/shard_map/all_to_all | solution.py:72
  343.7 0.9 convolution_bitcast_fusion.2
  344.6 0.9 subtract_bitcast_fusion.2
  346.0 39.9 %all_to_all.178 = f32[1,2,256,1,256]{4,3,1,0,2:T(1,128)S(1)} all-to-all(f32[1,2,256,1,256]{4,3,1,0,2:T(1,128)S(1)} %copy.203), channel_id=1, replica_groups=mesh['ctx'=128,'tp'=4] {'ctx'}, dimensions={2} | all-to-all | bytes 1048576 | tf_op jit(solution)/shard_map/all_to_all | solution.py:89
  391.6 40.8 %all_to_all.179 = f32[1,2,2,128,256]{4,2,1,0,3:T(2,128)S(1)} all-to-all(f32[1,2,2,128,256]{4,2,1,0,3:T(2,128)S(1)} %copy.216), channel_id=1, replica_groups=mesh['ctx'=128,'tp'=4] {'ctx'}, dimensions={3} | all-to-all | bytes 1048576 | tf_op jit(solution)/shard_map/all_to_all | solution.py:92
  434.5 0.9 pad_maximum_fusion.2
  436.2 64.0 %all_to_all.180 = f32[2,2,256,1,256]{4,3,1,0,2:T(1,128)S(1)} all-to-all(f32[2,2,256,1,256]{4,3,1,0,2:T(1,128)S(1)} %copy.217), channel_id=1, replica_groups=mesh['ctx'=128,'tp'=4] {'ctx'}, dimensions={2} | all-to-all | bytes 2097152 | tf_op jit(solution)/shard_map/all_to_all | solution.py:99
  500.7 0.8 fusion.410
  501.8 0.9 fusion.37
  503.0 0.9 fusion.33
  503.9 0.9 fusion.3
  504.8 1.0 multiply_subtract_fusion
  507.3 0.7 fusion.1
  508.0 0.7 fusion
  509.4 0.8 copy.231
  510.3 62.8 %all_to_all.181 = f32[2,2,2,128,256]{4,2,0,1,3:T(2,128)S(1)} all-to-all(f32[2,2,2,128,256]{4,2,0,1,3:T(2,128)S(1)} %copy.231), channel_id=1, replica_groups=mesh['ctx'=128,'tp'=4] {'ctx'}, dimensions={3} | all-to-all | bytes 2097152 | tf_op jit(solution)/shard_map/all_to_all | solution.py:113
  573.6 0.8 fusion.409
  575.1 1.1 fusion.21
  576.2 1.1 fusion.17
  577.3 0.8 copy.235
  578.1 9.0 all-to-all-start.11
  587.1 356.9 %psum.23 = f32[256]{0:T(256)} all-reduce(f32[256]{0:T(256)S(1)} %get-tuple-element.18), channel_id=1, replica_groups=mesh['ctx'=128,'tp'=4] {'ctx'}, use_global_device_ids=true, to_apply=%region_5.6 | all-reduce | flops 256 | bytes 2048 | tf_op jit(solution)/shard_map/psum | solution.py:163
  (107 shorter events, 31.1 us)
Async XLA Ops:
  1.5 0.8 copy-start.1
  1.6 0.9 copy-start.2
  3.5 44.6 %all-to-all-start = ((f32[2,1,128,256]{3,0,1,2:T(2,128)}), f32[2,1,128,256]{3,0,1,2:T(2,128)S(1)}, u32[]{:S(2)}, u32[]{:S(2)}) async-start(f32[2,1,128,256]{3,0,1,2:T(2,128)} %maximum_bitcast_fusion.3), calls=%async_computation | async-start | bytes 524288 | tf_op jit(solution)/shard_map/all_to_all | solution.py:72
  51.8 64.0 %all-to-all-start.1 = ((f32[2,2,256,1,256]{4,0,3,1,2:T(2,128)}), f32[2,2,256,1,256]{4,0,3,1,2:T(2,128)S(1)}, u32[]{:S(2)}, u32[]{:S(2)}) async-start(f32[2,2,256,1,256]{4,0,3,1,2:T(2,128)} %copy.171), calls=%async_computation.1 | async-start | bytes 2097152 | tf_op jit(solution)/shard_map/all_to_all | solution.py:89
  191.9 39.3 %all-to-all-start.3 = ((f32[1,2,256,1,256]{4,3,1,0,2:T(1,128)}), f32[1,2,256,1,256]{4,3,1,0,2:T(1,128)S(1)}, u32[]{:S(2)}, u32[]{:S(2)}) async-start(f32[1,2,256,1,256]{4,3,1,0,2:T(1,128)} %copy.186), calls=%async_computation.3 | async-start | bytes 1048576 | tf_op jit(solution)/shard_map/all_to_all | solution.py:99
  280.3 24.6 %copy-start = (bf16[128,256]{1,0:T(8,128)(2,1)S(1)}, bf16[128,256]{1,0:T(8,128)(2,1)}, u32[]{:S(2)}) copy-start(bf16[128,256]{1,0:T(8,128)(2,1)} %param.6) | copy-start | bytes 196612
  304.9 5.8 copy-start.3
  310.6 0.7 copy-start.4
  578.1 365.9 %all-to-all-start.11 = ((f32[2,128,1,256]{3,2,0,1:T(1,128)}), f32[2,128,1,256]{3,2,0,1:T(1,128)S(1)}, u32[]{:S(2)}, u32[]{:S(2)}) async-start(f32[2,128,1,256]{3,2,0,1:T(1,128)} %copy.235), calls=%async_computation.11 | async-start | bytes 524288 | tf_op jit(solution)/shard_map/all_to_all | solution.py:119
where the time goes:
time: 954 us; the launch traced here: 946 us
  blocking collectives  729 us (76%)
  waiting for transfers between devices  107 us (11%)
  starting transfers between devices  49.7 us (5%)
  matrix products  28.8 us (3%)
  local copies, waits for them, and re-layouts  22 us (2%)
    psum x1, blocking collectives, per_device(): grad_gain = lax.psum(jnp.sum(cot_f * gated_out * inv_rms, axis=0), 'ctx')  357 us
    all_to_all x2, blocking collectives, seq_inverse(): lax.all_to_all(twisted, 'ctx', split_axis=3, concat_axis=2, tiled=True)  103 us
    all_to_all x2, blocking collectives, seq_forward(): lax.all_to_all(spectra, 'ctx', split_axis=3, concat_axis=2, tiled=True)  103 us
    all_to_all x1, blocking collectives, seq_inverse(): lax.all_to_all(spectra, 'ctx', split_axis=2, concat_axis=3, tiled=True)  64 us
    all_to_all x1, waiting for transfers between devices, seq_forward(): lax.all_to_all(twisted, 'ctx', split_axis=2, concat_axis=3, tiled=True)  54.4 us
    all_to_all x1, blocking collectives, seq_forward(): lax.all_to_all(twisted, 'ctx', split_axis=2, concat_axis=3, tiled=True)  39.9 us
    all_to_all x1, waiting for transfers between devices, seq_inverse(): lax.all_to_all(spectra, 'ctx', split_axis=2, concat_axis=3, tiled=True)  30.2 us
    dot_general x40, matrix products, mix_sum(): return jnp.einsum(form, table, operand, precision=lax.Precision.HIGHEST)  28.8 us
  transfers between devices with their start and end apart: 4, of which 3 were waited for; matrix products, arithmetic and copies ran while one was open for 0% of the time, Pallas kernels for 0%

commit v1 on v0

v1 whole, which is shorter than its diff:
```python
import functools
import math

import jax
import jax.numpy as jnp
import ml_dtypes
import numpy as np
from jax import lax
from jax.experimental import pallas as pl
from jax.experimental.pallas import tpu as pltpu
from jax.sharding import Mesh, PartitionSpec as P

norm_eps = 1e-06
side = 128
length = side * side
channels = 1024
ctx_axes = ("yh", "z", "x")
ctx_sizes = (2, 16, 4)
tp_axes = ("yl", "core")
tp_sizes = (2, 2)
swap_axes = ("z", "yh", "x")
vmem_bytes = 40 * 1024 * 1024


def split_table(table):
    high = table.astype(np.float32).astype(ml_dtypes.bfloat16)
    low = (table - high.astype(np.float64)).astype(ml_dtypes.bfloat16)
    return np.stack([high, low])


def make_tables():
    order = [ctx_axes.index(name) for name in swap_axes]
    block = np.arange(side).reshape(ctx_sizes).transpose(order).reshape(-1)
    idx = np.arange(side)
    ang_a = 2.0 * math.pi * ((idx[:, None] + 0.25) * block[None, :] / side)
    cos_a, sin_a = np.cos(ang_a), np.sin(ang_a)
    first = np.concatenate([cos_a, sin_a], axis=0)
    scale = 1.0 / length / math.sqrt(length)
    last = np.concatenate([cos_a.T, sin_a.T], axis=1) * scale
    ang_t = 2.0 * math.pi * ((idx[:, None] + 0.25) * idx[None, :] / length)
    twist = np.stack([np.cos(ang_t), np.sin(ang_t)]).astype(np.float32)
    ang_b = 2.0 * math.pi * (idx[:, None] * idx[None, :] % side) / side
    cos_b, sin_b = np.cos(ang_b), np.sin(ang_b)
    ahead = np.block([[cos_b, sin_b], [-sin_b, cos_b]])
    back = np.block([[cos_b, -sin_b], [sin_b, cos_b]])
    return tuple(split_table(t) for t in (first, ahead, back, last)) + (twist,)


def halves(value):
    high = value.astype(jnp.bfloat16)
    low = (value - high.astype(jnp.float32)).astype(jnp.bfloat16)
    return high, low


def dot(left, right):
    return jnp.dot(left, right, preferred_element_type=jnp.float32)


def table_dot(table_ref, value):
    high, low = halves(value)
    return dot(table_ref[0], high) + (dot(table_ref[0], low) + dot(table_ref[1], high))


def dot_table(value, table_ref):
    high, low = halves(value)
    return dot(high, table_ref[0]) + (dot(low, table_ref[0]) + dot(high, table_ref[1]))


def forward_spectra(columns, first_ref, ahead_ref, twist_ref):
    count = len(columns)
    mid = table_dot(first_ref, jnp.concatenate(columns, axis=1))
    cos_t, sin_t = twist_ref[0], twist_ref[1]
    rows = []
    for u in range(count):
        real = mid[:side, u * side : (u + 1) * side]
        imag = mid[side:, u * side : (u + 1) * side]
        rows.append(
            jnp.concatenate([real * cos_t - imag * sin_t, real * sin_t + imag * cos_t], axis=1)
        )
    out = dot_table(jnp.concatenate(rows, axis=0), ahead_ref)
    return [
        (out[u * side : (u + 1) * side, :side], out[u * side : (u + 1) * side, side:])
        for u in range(count)
    ]


def inverse_columns(spectra, back_ref, last_ref, twist_ref):
    count = len(spectra)
    mid = dot_table(
        jnp.concatenate([jnp.concatenate(pair, axis=1) for pair in spectra], axis=0), back_ref
    )
    cos_t, sin_t = twist_ref[0], twist_ref[1]
    cols = []
    for u in range(count):
        real = mid[u * side : (u + 1) * side, :side]
        imag = mid[u * side : (u + 1) * side, side:]
        cols.append(
            jnp.concatenate([real * cos_t + imag * sin_t, imag * cos_t - real * sin_t], axis=0)
        )
    return table_dot(last_ref, jnp.concatenate(cols, axis=1))


def product(left, right):
    return (left[0] * right[0] - left[1] * right[1], left[0] * right[1] + left[1] * right[0])


def conj_product(left, right):
    return (left[0] * right[0] + left[1] * right[1], left[0] * right[1] - left[1] * right[0])


def every(start, stride):
    return pl.ds(start, side, stride=stride)


def send_inputs_kernel(key_ref, value_ref, filt_ref, out_ref):
    mixed = key_ref[...].astype(jnp.float32) * value_ref[...].astype(jnp.float32)
    filt = filt_ref[...]
    for h in range(2):
        cols = slice(h * side, (h + 1) * side)
        out_ref[every(h, 4), :] = filt[:, cols].T
        out_ref[every(2 + h, 4), :] = mixed[:, cols].T


def flip_gates_kernel(query_ref, cot_ref, query_t_ref, cot_t_ref):
    query = query_ref[...].astype(jnp.float32)
    cot = cot_ref[...].astype(jnp.float32)
    for h in range(2):
        cols = slice(h * side, (h + 1) * side)
        query_t_ref[cols, :] = query[:, cols].T
        cot_t_ref[cols, :] = cot[:, cols].T


def conv_kernel(got_ref, first_ref, ahead_ref, back_ref, last_ref, twist_ref, out_ref, spec_ref):
    columns = [got_ref[every(u, 4), :] for u in range(4)]
    spectra = forward_spectra(columns, first_ref, ahead_ref, twist_ref)
    for u in range(4):
        spec_ref[u, 0] = spectra[u][0]
        spec_ref[u, 1] = spectra[u][1]
    both = [product(spectra[h], spectra[2 + h]) for h in range(2)]
    conv = inverse_columns(both, back_ref, last_ref, twist_ref)
    for h in range(2):
        out_ref[every(h, 2), :] = conv[:, h * side : (h + 1) * side]


def row_sums_kernel(conv_ref, query_t_ref, cot_t_ref, gain_ref, out_ref):
    squares = jnp.zeros((1, side), jnp.float32)
    dots = jnp.zeros((1, side), jnp.float32)
    for h in range(2):
        cols = slice(h * side, (h + 1) * side)
        gated = conv_ref[every(h, 2), :] * query_t_ref[cols, :]
        squares = squares + jnp.sum(gated * gated, axis=0, keepdims=True)
        scaled = cot_t_ref[cols, :] * gain_ref[cols, :]
        dots = dots + jnp.sum(scaled * gated, axis=0, keepdims=True)
    out_ref[0:1, :] = squares
    out_ref[1:2, :] = dots


def row_scalars(sums_ref):
    squares = sums_ref[0, 0:1, :]
    dots = sums_ref[0, 1:2, :]
    for t in range(1, 4):
        squares = squares + sums_ref[t, 0:1, :]
        dots = dots + sums_ref[t, 1:2, :]
    inv_rms = lax.rsqrt(squares * (1.0 / channels) + norm_eps)
    return inv_rms, dots * (1.0 / channels)


def d_conv_kernel(conv_ref, query_t_ref, cot_t_ref, gain_ref, sums_ref, out_ref):
    inv_rms, row_dot = row_scalars(sums_ref)
    pull = inv_rms * inv_rms * inv_rms * row_dot
    gains = []
    for h in range(2):
        cols = slice(h * side, (h + 1) * side)
        query = query_t_ref[cols, :]
        cot = cot_t_ref[cols, :]
        gated = conv_ref[every(h, 2), :] * query
        scaled = cot * gain_ref[cols, :]
        out_ref[every(h, 3), :] = (inv_rms * scaled - gated * pull) * query
        gains.append(jnp.sum(cot * gated * inv_rms, axis=1, keepdims=True))
    lane = lax.broadcasted_iota(jnp.int32, (side, side), 1)
    out_ref[every(2, 3), :] = jnp.where(lane < side // 2, gains[0], gains[1])


def row_outputs_kernel(
    conv_ref, query_t_ref, cot_t_ref, gain_ref, sums_ref, gain_row_ref, output_ref, grad_query_ref
):
    inv_rms, row_dot = row_scalars(sums_ref)
    pull = inv_rms * inv_rms * inv_rms * row_dot
    for h in range(2):
        cols = slice(h * side, (h + 1) * side)
        conv = conv_ref[every(h, 2), :]
        gated = conv * query_t_ref[cols, :]
        scaled = cot_t_ref[cols, :] * gain_ref[cols, :]
        normed = (gated * inv_rms).T
        output_ref[:, cols] = (normed * gain_row_ref[:, cols]).astype(jnp.bfloat16)
        grad = (inv_rms * scaled - gated * pull) * conv
        grad_query_ref[:, cols] = grad.T.astype(jnp.bfloat16)


def corr_kernel(
    got_ref, spec_ref, first_ref, ahead_ref, back_ref, last_ref, twist_ref, out_ref
):
    columns = [got_ref[every(h, 3), :] for h in range(2)]
    spectra = forward_spectra(columns, first_ref, ahead_ref, twist_ref)
    pairs = [
        conj_product((spec_ref[u, 0], spec_ref[u, 1]), spectra[u % 2]) for u in range(4)
    ]
    result = inverse_columns(pairs, back_ref, last_ref, twist_ref)
    for u in range(4):
        out_ref[every(u, 5), :] = result[:, u * side : (u + 1) * side]
    gain_sum = jnp.sum(got_ref[every(2, 3), :], axis=0, keepdims=True)
    out_ref[every(4, 5), :] = jnp.broadcast_to(gain_sum, (side, side))


def last_outputs_kernel(
    got_ref, key_ref, value_ref, grad_key_ref, grad_value_ref, grad_filter_ref, grad_gain_ref
):
    gains = got_ref[every(4, 5), :].T
    for h in range(2):
        cols = slice(h * side, (h + 1) * side)
        d_mixed = got_ref[every(h, 5), :].T
        value = value_ref[:, cols].astype(jnp.float32)
        key = key_ref[:, cols].astype(jnp.float32)
        grad_key_ref[:, cols] = (d_mixed * value).astype(jnp.bfloat16)
        grad_value_ref[:, cols] = (d_mixed * key).astype(jnp.bfloat16)
        grad_filter_ref[:, cols] = got_ref[every(2 + h, 5), :].T
        grad_gain_ref[:, cols] = gains[h * (side // 2) : h * (side // 2) + 1, :]


def call(kernel, outs, *operands, flops=0):
    moved = sum(math.prod(o.shape) * o.dtype.itemsize for o in operands)
    moved += sum(math.prod(o.shape) * o.dtype.itemsize for o in outs)
    result = pl.pallas_call(
        kernel,
        out_shape=outs,
        compiler_params=pltpu.CompilerParams(vmem_limit_bytes=vmem_bytes),
        cost_estimate=pl.CostEstimate(flops=flops, bytes_accessed=moved, transcendentals=0),
    )(*operands)
    return result


def f32(*shape):
    return jax.ShapeDtypeStruct(shape, jnp.float32)


def bf16(*shape):
    return jax.ShapeDtypeStruct(shape, jnp.bfloat16)


def swap(sent, rows):
    got = lax.all_to_all(
        sent.reshape(side, 1, rows * side), swap_axes, split_axis=0, concat_axis=0, tiled=True
    )
    return got.reshape(side * rows, side)


def per_device(gate_query, key_proj, value_proj, long_filter, out_gain, cotangent):
    first, ahead, back, last, twist = (jnp.asarray(t) for t in make_tables())
    wide = 2 * side
    gain_row = out_gain.reshape(1, wide)
    gain_col = jnp.broadcast_to(out_gain[:, None], (wide, side))

    (sent,) = call(send_inputs_kernel, (f32(4 * side, side),), key_proj, value_proj, long_filter)
    got = swap(sent, 4)
    query_t, cot_t = call(
        flip_gates_kernel, (f32(wide, side), f32(wide, side)), gate_query, cotangent
    )
    sent, spectra = call(
        conv_kernel,
        (f32(wide, side), f32(4, 2, side, side)),
        got,
        first,
        ahead,
        back,
        last,
        twist,
    )
    conv_t = swap(sent, 2)
    (sums,) = call(row_sums_kernel, (f32(2, side),), conv_t, query_t, cot_t, gain_col)
    sums = lax.all_gather(sums, tp_axes)
    (sent,) = call(d_conv_kernel, (f32(3 * side, side),), conv_t, query_t, cot_t, gain_col, sums)
    got = swap(sent, 3)
    output, grad_query = call(
        row_outputs_kernel,
        (bf16(side, wide), bf16(side, wide)),
        conv_t,
        query_t,
        cot_t,
        gain_col,
        sums,
        gain_row,
    )
    (sent,) = call(
        corr_kernel,
        (f32(5 * side, side),),
        got,
        spectra,
        first,
        ahead,
        back,
        last,
        twist,
    )
    got = swap(sent, 5)
    grad_key, grad_value, grad_filter, grad_gain = call(
        last_outputs_kernel,
        (bf16(side, wide), bf16(side, wide), f32(side, wide), f32(1, wide)),
        got,
        key_proj,
        value_proj,
    )
    return (output, grad_query, grad_key, grad_value, grad_filter, grad_gain.reshape(wide))


def solution(mesh):
    fine = Mesh(mesh.devices.reshape(ctx_sizes + tp_sizes), ctx_axes + tp_axes)
    both = P(ctx_axes, tp_axes)
    return jax.shard_map(
        per_device,
        mesh=fine,
        in_specs=(both, both, both, both, P(tp_axes), both),
        out_specs=(both, both, both, both, both, P(tp_axes)),
        check_vma=False,
    )
```

time: 954 us -> 145 us (0.15)
  blocking collectives: 729 us -> 77.2 us
  waiting for transfers between devices: 107 us -> 41 us
  starting transfers between devices: 49.7 us -> 15.4 us
  matrix products: 28.8 us -> 0 us
  local copies, waits for them, and re-layouts: 22 us -> 2.72 us
    psum x3 -> x0, blocking collectives: 369 us -> none  [the longest x1 357 us: per_device(): grad_gain = lax.psum(jnp.sum(cot_f * gated_out * inv_rms, axis=0), 'ctx')]
    all_to_all x8 -> x2, blocking collectives: 360 us -> 72.2 us  [swap(): lax.all_to_all(sent.reshape(side, 1, rows * side), swap_axes, split_axis=...]
    all_to_all x4 -> x2, waiting for transfers between devices: 107 us -> 41 us  [swap(): lax.all_to_all(sent.reshape(side, 1, rows * side), swap_axes, split_axis=...]
    all_to_all x4 -> x2, starting transfers between devices: 49.7 us -> 15.4 us  [swap(): lax.all_to_all(sent.reshape(side, 1, rows * side), swap_axes, split_axis=...]
    dot_general x40 -> x0, matrix products: 28.8 us -> none  [mix_sum(): return jnp.einsum(form, table, operand, precision=lax.Precision.HIGHEST)]
  transfers between devices with their start and end apart: 4 -> 2, of which waited for: 3 -> 2; matrix products, arithmetic and copies ran while one was open for 0% -> 0% of each run, Pallas kernels for 0% -> 1%
where the time goes in v1:
time: 145 us; the launch traced here: 143 us
  blocking collectives  77.2 us (53%)
  waiting for transfers between devices  41 us (28%)
  starting transfers between devices  15.4 us (11%)
  Pallas kernels  6.06 us (4%)
  local copies, waits for them, and re-layouts  2.72 us (2%)
    all_to_all x2, blocking collectives, swap(): lax.all_to_all(sent.reshape(side, 1, rows * side), swap_axes, split_axis=...  72.2 us
    all_to_all x2, waiting for transfers between devices, swap(): lax.all_to_all(sent.reshape(side, 1, rows * side), swap_axes, split_axis=...  41 us
    all_to_all x2, starting transfers between devices, swap(): lax.all_to_all(sent.reshape(side, 1, rows * side), swap_axes, split_axis=...  15.4 us
    pallas_call x8, Pallas kernels, call(): pl.pallas_call(kernel, out_shape=outs, compiler_params=pltpu.CompilerPara...  6.06 us
    all_gather x1, blocking collectives, per_device(): sums = lax.all_gather(sums, tp_axes)  5.07 us
  transfers between devices with their start and end apart: 2, of which 2 were waited for; matrix products, arithmetic and copies ran while one was open for 0% of the time, Pallas kernels for 1%

profile of v1, /device:TPU:24, one launch (start us, length us, event | category | flops | bytes accessed | tf_op | source)
XLA Modules:
  0.0 143.2 jit_solution(17398268254426009968)
XLA Ops:
  0.6 0.0 copy-start.5
  0.6 0.8 copy-done.5
  1.5 0.0 copy-start.7
  1.5 0.8 copy-done.7
  2.3 0.0 copy-start.9
  2.3 0.9 copy-done.9
  3.2 0.0 copy-start.2
  3.2 0.0 copy-start.3
  3.2 0.0 copy-start.4
  3.2 0.1 shard_map.154
  3.4 0.0 copy-start
  3.4 0.0 copy-start.1
  3.4 44.7 %all_to_all.20 = f32[128,1,512]{2,1,0:T(1,128)S(1)} all-to-all(f32[128,1,512]{2,1,0:T(1,128)S(1)} %bitcast.15), channel_id=1, replica_groups=mesh['yh'=2,'z'=16,'x'=4,'yl'=2,'core'=2] {'z','yh','x'}, dimensions={0} | all-to-all | bytes 524288 | tf_op jit(solution)/shard_map/all_to_all | solution.py:251
  48.1 0.0 copy-done.2
  48.1 0.0 copy-done.3
  48.1 0.0 copy-done.4
  48.1 0.0 copy-done
  48.1 0.0 copy-done.1
  48.1 2.0 %shard_map.155 = (f32[256,128]{1,0:T(8,128)}, f32[4,2,128,128]{3,2,1,0:T(8,128)S(1)}) custom-call(f32[512,128]{1,0:T(8,128)S(1)} %bitcast.16, bf16[2,256,128]{2,1,0:T(8,128)(2,1)S(1)} %copy-done.4, bf16[2,256,256]{2,1,0:T(8,128)(2,1)S(1)} %copy-done.1, bf16[2,256,256]{2,1,0:T(8,128)(2,1)S(1)} %copy-done, bf16[2,128,256]{2,1,0:T(8,128)(2,1)S(1)} %copy-done.3, ...), custom_call_target="tpu_custom_call" | custom-call | bytes 1835008 | tf_op jit(solution)/shard_map/pallas_call | solution.py:233
  50.1 0.0 copy-start.10
  50.1 0.0 copy-start.11
  50.1 7.7 %all-to-all-start.1 = ((f32[128,1,256]{2,1,0:T(1,128)}), f32[128,1,256]{2,1,0:T(1,128)S(1)}, u32[]{:S(2)}, u32[]{:S(2)}) async-start(f32[128,1,256]{2,1,0:T(1,128)} %bitcast.2), calls=%async_computation.1 | async-start | bytes 262144 | tf_op jit(solution)/shard_map/all_to_all | solution.py:251
  57.8 0.0 copy-done.10
  57.8 0.0 copy-done.11
  57.8 0.0 copy-start.12
  57.8 0.1 shard_map.156
  57.9 16.8 %all-to-all-done.1 = f32[128,1,256]{2,1,0:T(1,128)S(1)} async-done(((f32[128,1,256]{2,1,0:T(1,128)}), f32[128,1,256]{2,1,0:T(1,128)S(1)}, u32[]{:S(2)}, u32[]{:S(2)}) %all-to-all-start.1) | async-done | bytes 131104 | tf_op jit(solution)/shard_map/all_to_all | solution.py:251
  74.7 0.0 copy-done.12
  74.7 0.1 broadcast_in_dim.2.gain_ref
  74.8 5.1 %all-gather.1.sums_ref = f32[4,2,128]{2,1,0:T(2,128)S(1)} all-gather(f32[1,2,128]{2,1,0:T(2,128)S(1)} %bitcast.20), channel_id=2, replica_groups=mesh['yh'=2,'z'=16,'x'=4,'yl'=2,'core'=2] {'yl','core'}, dimensions={0}, use_global_device_ids=true | all-gather | bytes 5120 | tf_op jit(solution)/shard_map/all_gather | solution.py:280
  79.9 0.1 shard_map.159
  80.0 27.5 %all_to_all.21 = f32[128,1,384]{2,1,0:T(1,128)S(1)} all-to-all(f32[128,1,384]{2,1,0:T(1,128)S(1)} %bitcast.17), channel_id=1, replica_groups=mesh['yh'=2,'z'=16,'x'=4,'yl'=2,'core'=2] {'z','yh','x'}, dimensions={0} | all-to-all | bytes 393216 | tf_op jit(solution)/shard_map/all_to_all | solution.py:251
  107.5 2.1 %shard_map.160 = f32[640,128]{1,0:T(8,128)} custom-call(f32[384,128]{1,0:T(8,128)S(1)} %bitcast.18, f32[4,2,128,128]{3,2,1,0:T(8,128)S(1)} %get-tuple-element.21.spec_ref, bf16[2,256,128]{2,1,0:T(8,128)(2,1)S(1)} %copy-done.4, bf16[2,256,256]{2,1,0:T(8,128)(2,1)S(1)} %copy-done.1, bf16[2,256,256]{2,1,0:T(8,128)(2,1)S(1)} %copy-done, ...), custom_call_target="tpu_custom_call" | custom-call | bytes 1966080 | tf_op jit(solution)/shard_map/pallas_call | solution.py:233
  109.6 7.7 %all-to-all-start.3 = ((f32[128,1,640]{2,1,0:T(1,128)}), f32[128,1,640]{2,1,0:T(1,128)S(1)}, u32[]{:S(2)}, u32[]{:S(2)}) async-start(f32[128,1,640]{2,1,0:T(1,128)} %bitcast.8), calls=%async_computation.3 | async-start | bytes 655360 | tf_op jit(solution)/shard_map/all_to_all | solution.py:251
  117.3 0.0 copy-start.6
  117.3 0.0 copy-start.8
  117.3 0.8 shard_map.158
  118.1 24.3 %all-to-all-done.3 = f32[128,1,640]{2,1,0:T(1,128)S(1)} async-done(((f32[128,1,640]{2,1,0:T(1,128)}), f32[128,1,640]{2,1,0:T(1,128)S(1)}, u32[]{:S(2)}, u32[]{:S(2)}) %all-to-all-start.3) | async-done | bytes 327712 | tf_op jit(solution)/shard_map/all_to_all | solution.py:251
  142.4 0.0 copy-done.6
  142.4 0.0 copy-done.8
  142.4 0.8 shard_map.161
  (1 shorter events, 0.0 us)
Async XLA Ops:
  0.6 0.8 copy-start.5
  1.5 0.8 copy-start.7
  2.3 0.9 copy-start.9
  3.2 44.9 %copy-start.2 = (f32[2,128,128]{2,1,0:T(8,128)S(1)}, f32[2,128,128]{2,1,0:T(8,128)}, u32[]{:S(2)}) copy-start(f32[2,128,128]{2,1,0:T(8,128)} %constant.14.clone.twist_ref) | copy-start | bytes 393220
  3.2 44.9 %copy-start.3 = (bf16[2,128,256]{2,1,0:T(8,128)(2,1)S(1)}, bf16[2,128,256]{2,1,0:T(8,128)(2,1)}, u32[]{:S(2)}) copy-start(bf16[2,128,256]{2,1,0:T(8,128)(2,1)} %constant.13.clone.last_ref) | copy-start | bytes 393220
  3.2 44.9 %copy-start.4 = (bf16[2,256,128]{2,1,0:T(8,128)(2,1)S(1)}, bf16[2,256,128]{2,1,0:T(8,128)(2,1)}, u32[]{:S(2)}) copy-start(bf16[2,256,128]{2,1,0:T(8,128)(2,1)} %constant.10.clone.first_ref) | copy-start | bytes 393220
  3.4 44.7 %copy-start = (bf16[2,256,256]{2,1,0:T(8,128)(2,1)S(1)}, bf16[2,256,256]{2,1,0:T(8,128)(2,1)}, u32[]{:S(2)}) copy-start(bf16[2,256,256]{2,1,0:T(8,128)(2,1)} %constant.12.clone.back_ref) | copy-start | bytes 786436
  3.4 44.7 %copy-start.1 = (bf16[2,256,256]{2,1,0:T(8,128)(2,1)S(1)}, bf16[2,256,256]{2,1,0:T(8,128)(2,1)}, u32[]{:S(2)}) copy-start(bf16[2,256,256]{2,1,0:T(8,128)(2,1)} %constant.11.clone.ahead_ref) | copy-start | bytes 786436
  50.1 7.7 %copy-start.10 = (bf16[128,256]{1,0:T(8,128)(2,1)S(1)}, bf16[128,256]{1,0:T(8,128)(2,1)}, u32[]{:S(2)}) copy-start(bf16[128,256]{1,0:T(8,128)(2,1)} %query_ref.1) | copy-start | bytes 196612
  50.1 7.7 %copy-start.11 = (bf16[128,256]{1,0:T(8,128)(2,1)S(1)}, bf16[128,256]{1,0:T(8,128)(2,1)}, u32[]{:S(2)}) copy-start(bf16[128,256]{1,0:T(8,128)(2,1)} %cot_ref.1) | copy-start | bytes 196612
  50.1 24.6 %all-to-all-start.1 = ((f32[128,1,256]{2,1,0:T(1,128)}), f32[128,1,256]{2,1,0:T(1,128)S(1)}, u32[]{:S(2)}, u32[]{:S(2)}) async-start(f32[128,1,256]{2,1,0:T(1,128)} %bitcast.2), calls=%async_computation.1 | async-start | bytes 262144 | tf_op jit(solution)/shard_map/all_to_all | solution.py:251
  57.8 16.9 %copy-start.12 = (f32[256]{0:T(256)S(1)}, f32[256]{0:T(256)}, u32[]{:S(2)}) copy-start(f32[256]{0:T(256)} %param.15) | copy-start | bytes 3076
  109.6 32.8 %all-to-all-start.3 = ((f32[128,1,640]{2,1,0:T(1,128)}), f32[128,1,640]{2,1,0:T(1,128)S(1)}, u32[]{:S(2)}, u32[]{:S(2)}) async-start(f32[128,1,640]{2,1,0:T(1,128)} %bitcast.8), calls=%async_computation.3 | async-start | bytes 655360 | tf_op jit(solution)/shard_map/all_to_all | solution.py:251
  117.3 25.1 %copy-start.6 = (bf16[128,256]{1,0:T(8,128)(2,1)S(1)}, bf16[128,256]{1,0:T(8,128)(2,1)}, u32[]{:S(2)}) copy-start(bf16[128,256]{1,0:T(8,128)(2,1)} %key_ref.3) | copy-start | bytes 196612
  117.3 25.1 %copy-start.8 = (bf16[128,256]{1,0:T(8,128)(2,1)S(1)}, bf16[128,256]{1,0:T(8,128)(2,1)}, u32[]{:S(2)}) copy-start(bf16[128,256]{1,0:T(8,128)(2,1)} %value_ref.3) | copy-start | bytes 196612

commit v2 on v1

v2 whole, which is shorter than its diff:
```python
import math

import jax
import jax.numpy as jnp
import numpy as np
from jax import lax
from jax.experimental import pallas as pl
from jax.experimental.pallas import tpu as pltpu
from jax.sharding import PartitionSpec as P

norm_eps = 1e-06
side = 128
length = side * side
channels = 1024
ctx_sizes = (2, 16, 4)
vmem_bytes = 40 * 1024 * 1024


def swap_order():
    grid = np.arange(side).reshape(ctx_sizes).transpose(1, 2, 0)
    return np.roll(grid, (8, 2, 1), axis=(0, 1, 2)).reshape(-1).tolist()


def make_tables():
    block = np.array(swap_order())
    idx = np.arange(side)
    ang_a = 2.0 * math.pi * ((idx[:, None] + 0.25) * block[None, :] / side)
    cos_a, sin_a = np.cos(ang_a), np.sin(ang_a)
    first = np.concatenate([cos_a, sin_a], axis=0)
    scale = 1.0 / length / math.sqrt(length)
    last = np.concatenate([cos_a.T, sin_a.T], axis=1) * scale
    ang_t = 2.0 * math.pi * ((idx[:, None] + 0.25) * idx[None, :] / length)
    twist = np.stack([np.cos(ang_t), np.sin(ang_t)]).astype(np.float32)
    ang_b = 2.0 * math.pi * (idx[:, None] * idx[None, :] % side) / side
    cos_b, sin_b = np.cos(ang_b), np.sin(ang_b)
    ahead = np.block([[cos_b, sin_b], [-sin_b, cos_b]])
    back = np.block([[cos_b, -sin_b], [sin_b, cos_b]])
    return tuple(t.astype(np.float32) for t in (first, ahead, back, last)) + (twist,)


def halves(value):
    high = value.astype(jnp.bfloat16)
    low = (value - high.astype(jnp.float32)).astype(jnp.bfloat16)
    return high, low


def dot(left, right):
    return jnp.dot(left, right, preferred_element_type=jnp.float32)


def split_kernel(*refs):
    count = len(refs) // 3
    for i in range(count):
        high, low = halves(refs[i][...])
        refs[count + 2 * i][...] = high
        refs[count + 2 * i + 1][...] = low


def exact_dot(left, right):
    (left_high, left_low), (right_high, right_low) = left, right
    return dot(left_high, right_high) + (dot(left_high, right_low) + dot(left_low, right_high))


def load(pair):
    return pair[0][...], pair[1][...]


def forward_spectra(columns, first, ahead, twist_ref):
    count = len(columns)
    mid = exact_dot(load(first), halves(jnp.concatenate(columns, axis=1)))
    cos_t, sin_t = twist_ref[0], twist_ref[1]
    rows = []
    for u in range(count):
        real = mid[:side, u * side : (u + 1) * side]
        imag = mid[side:, u * side : (u + 1) * side]
        rows.append(
            jnp.concatenate([real * cos_t - imag * sin_t, real * sin_t + imag * cos_t], axis=1)
        )
    out = exact_dot(halves(jnp.concatenate(rows, axis=0)), load(ahead))
    return [
        (out[u * side : (u + 1) * side, :side], out[u * side : (u + 1) * side, side:])
        for u in range(count)
    ]


def inverse_columns(spectra, back, last, twist_ref):
    count = len(spectra)
    stacked = jnp.concatenate([jnp.concatenate(pair, axis=1) for pair in spectra], axis=0)
    mid = exact_dot(halves(stacked), load(back))
    cos_t, sin_t = twist_ref[0], twist_ref[1]
    cols = []
    for u in range(count):
        real = mid[u * side : (u + 1) * side, :side]
        imag = mid[u * side : (u + 1) * side, side:]
        cols.append(
            jnp.concatenate([real * cos_t + imag * sin_t, imag * cos_t - real * sin_t], axis=0)
        )
    return exact_dot(load(last), halves(jnp.concatenate(cols, axis=1)))


def product(left, right):
    return (left[0] * right[0] - left[1] * right[1], left[0] * right[1] + left[1] * right[0])


def conj_product(left, right):
    return (left[0] * right[0] + left[1] * right[1], left[0] * right[1] - left[1] * right[0])


def every(start, stride):
    return pl.ds(start, side, stride=stride)


def send_inputs_kernel(key_hbm, value_hbm, filt_hbm, out_ref, key_ref, value_ref, filt_ref, sems):
    pairs = ((key_hbm, key_ref), (value_hbm, value_ref), (filt_hbm, filt_ref))
    copies = [pltpu.make_async_copy(a, b, sems.at[i]) for i, (a, b) in enumerate(pairs)]
    for copy in copies:
        copy.start()
    for copy in copies:
        copy.wait()
    mixed = key_ref[...].astype(jnp.float32) * value_ref[...].astype(jnp.float32)
    filt = filt_ref[...]
    for h in range(2):
        cols = slice(h * side, (h + 1) * side)
        out_ref[every(h, 4), :] = filt[:, cols].T
        out_ref[every(2 + h, 4), :] = mixed[:, cols].T


def flip_gates_kernel(query_ref, cot_ref, gain_ref, query_t_ref, cot_t_ref, scaled_t_ref):
    query = query_ref[...].astype(jnp.float32)
    cot = cot_ref[...].astype(jnp.float32)
    scaled = cot * gain_ref[...]
    for h in range(2):
        cols = slice(h * side, (h + 1) * side)
        query_t_ref[cols, :] = query[:, cols].T
        cot_t_ref[cols, :] = cot[:, cols].T
        scaled_t_ref[cols, :] = scaled[:, cols].T


def conv_kernel(got_ref, *refs):
    first, ahead, back, last = (refs[i : i + 2] for i in range(0, 8, 2))
    twist_ref, out_ref, spec_ref = refs[8:]
    columns = [got_ref[every(u, 4), :] for u in range(4)]
    spectra = forward_spectra(columns, first, ahead, twist_ref)
    for u in range(4):
        spec_ref[u, 0] = spectra[u][0]
        spec_ref[u, 1] = spectra[u][1]
    both = [product(spectra[h], spectra[2 + h]) for h in range(2)]
    conv = inverse_columns(both, back, last, twist_ref)
    for h in range(2):
        out_ref[every(h, 2), :] = conv[:, h * side : (h + 1) * side]


def row_sums_kernel(conv_ref, query_t_ref, scaled_t_ref, out_ref):
    squares = jnp.zeros((1, side), jnp.float32)
    dots = jnp.zeros((1, side), jnp.float32)
    for h in range(2):
        cols = slice(h * side, (h + 1) * side)
        gated = conv_ref[every(h, 2), :] * query_t_ref[cols, :]
        squares = squares + jnp.sum(gated * gated, axis=0, keepdims=True)
        dots = dots + jnp.sum(scaled_t_ref[cols, :] * gated, axis=0, keepdims=True)
    out_ref[0:1, :] = squares
    out_ref[1:2, :] = dots


def row_scalars(sums_ref):
    squares = sums_ref[0, 0:1, :]
    dots = sums_ref[0, 1:2, :]
    for t in range(1, 4):
        squares = squares + sums_ref[t, 0:1, :]
        dots = dots + sums_ref[t, 1:2, :]
    inv_rms = lax.rsqrt(squares * (1.0 / channels) + norm_eps)
    return inv_rms, dots * (1.0 / channels)


def d_conv_kernel(conv_ref, query_t_ref, cot_t_ref, scaled_t_ref, sums_ref, out_ref):
    inv_rms, row_dot = row_scalars(sums_ref)
    pull = inv_rms * inv_rms * inv_rms * row_dot
    parts = []
    for h in range(2):
        cols = slice(h * side, (h + 1) * side)
        query = query_t_ref[cols, :]
        cot = cot_t_ref[cols, :]
        gated = conv_ref[every(h, 2), :] * query
        scaled = scaled_t_ref[cols, :]
        out_ref[every(h, 3), :] = (inv_rms * scaled - gated * pull) * query
        part = jnp.sum(cot * gated * inv_rms, axis=1, keepdims=True)
        parts.append(jnp.broadcast_to(part, (side, side)).T)
    number = lax.broadcasted_iota(jnp.int32, (side, side), 0)
    out_ref[every(2, 3), :] = jnp.where((number & 2) == 0, parts[0], parts[1])


def row_outputs_kernel(
    conv_ref,
    query_t_ref,
    scaled_t_ref,
    sums_ref,
    gain_ref,
    got_ref,
    output_ref,
    grad_query_ref,
    gain_half_ref,
):
    inv_rms, row_dot = row_scalars(sums_ref)
    pull = inv_rms * inv_rms * inv_rms * row_dot
    for h in range(2):
        cols = slice(h * side, (h + 1) * side)
        conv = conv_ref[every(h, 2), :]
        gated = conv * query_t_ref[cols, :]
        scaled = scaled_t_ref[cols, :]
        normed = (gated * inv_rms).T
        output_ref[:, cols] = (normed * gain_ref[:, cols]).astype(jnp.bfloat16)
        grad = (inv_rms * scaled - gated * pull) * conv
        grad_query_ref[:, cols] = grad.T.astype(jnp.bfloat16)
    gain_half_ref[...] = jnp.sum(got_ref[every(2, 3), :], axis=0, keepdims=True)


def corr_kernel(got_ref, spec_ref, *refs):
    first, ahead, back, last = (refs[i : i + 2] for i in range(0, 8, 2))
    twist_ref, out_ref = refs[8:]
    columns = [got_ref[every(h, 3), :] for h in range(2)]
    spectra = forward_spectra(columns, first, ahead, twist_ref)
    pairs = [
        conj_product((spec_ref[u, 0], spec_ref[u, 1]), spectra[u % 2]) for u in range(4)
    ]
    result = inverse_columns(pairs, back, last, twist_ref)
    for u in range(4):
        out_ref[every(u, 4), :] = result[:, u * side : (u + 1) * side]


def last_outputs_kernel(
    got_ref, key_ref, value_ref, grad_key_ref, grad_value_ref, grad_filter_ref
):
    for h in range(2):
        cols = slice(h * side, (h + 1) * side)
        d_mixed = got_ref[every(h, 4), :].T
        value = value_ref[:, cols].astype(jnp.float32)
        key = key_ref[:, cols].astype(jnp.float32)
        grad_key_ref[:, cols] = (d_mixed * value).astype(jnp.bfloat16)
        grad_value_ref[:, cols] = (d_mixed * key).astype(jnp.bfloat16)
        grad_filter_ref[:, cols] = got_ref[every(2 + h, 4), :].T


def call(kernel, outs, *operands, limit=vmem_bytes, **options):
    moved = sum(math.prod(o.shape) * o.dtype.itemsize for o in operands)
    moved += sum(math.prod(o.shape) * o.dtype.itemsize for o in outs)
    result = pl.pallas_call(
        kernel,
        out_shape=outs,
        compiler_params=pltpu.CompilerParams(vmem_limit_bytes=limit),
        cost_estimate=pl.CostEstimate(flops=0, bytes_accessed=moved, transcendentals=0),
        **options,
    )(*operands)
    return result


def f32(*shape):
    return jax.ShapeDtypeStruct(shape, jnp.float32)


def bf16(*shape):
    return jax.ShapeDtypeStruct(shape, jnp.bfloat16)


def swap(sent, rows):
    shape = (side, 1, rows * side) if rows == 3 else (side, rows, side)
    got = lax.all_to_all(
        sent.reshape(shape),
        "ctx",
        split_axis=0,
        concat_axis=0,
        axis_index_groups=[swap_order()],
        tiled=True,
    )
    return got.reshape(side * rows, side)


def per_device(gate_query, key_proj, value_proj, long_filter, out_gain, cotangent):
    *tables, twist = (jnp.asarray(t) for t in make_tables())
    wide = 2 * side
    gain = out_gain.reshape(1, wide)

    in_hbm = pl.BlockSpec(memory_space=pltpu.HBM)
    (sent,) = call(
        send_inputs_kernel,
        (f32(4 * side, side),),
        key_proj,
        value_proj,
        long_filter,
        limit=None,
        in_specs=[in_hbm] * 3,
        scratch_shapes=[
            pltpu.VMEM((side, wide), jnp.bfloat16),
            pltpu.VMEM((side, wide), jnp.bfloat16),
            pltpu.VMEM((side, wide), jnp.float32),
            pltpu.SemaphoreType.DMA((3,)),
        ],
    )
    got = swap(sent, 4)
    tables = call(
        split_kernel, tuple(bf16(*t.shape) for t in tables for _ in range(2)), *tables
    )
    query_t, cot_t, scaled_t = call(
        flip_gates_kernel, (f32(wide, side),) * 3, gate_query, cotangent, gain
    )
    sent, spectra = call(
        conv_kernel,
        (f32(wide, side), f32(4, 2, side, side)),
        got,
        *tables,
        twist,
    )
    conv_t = swap(sent, 2)
    (sums,) = call(row_sums_kernel, (f32(2, side),), conv_t, query_t, scaled_t)
    sums = lax.all_gather(sums, "tp")
    (sent,) = call(d_conv_kernel, (f32(3 * side, side),), conv_t, query_t, cot_t, scaled_t, sums)
    got = swap(sent, 3)
    output, grad_query, gain_half = call(
        row_outputs_kernel,
        (bf16(side, wide), bf16(side, wide), f32(1, side)),
        conv_t,
        query_t,
        scaled_t,
        sums,
        gain,
        got,
    )
    other_half = lax.ppermute(gain_half, "ctx", [(i, i ^ 1) for i in range(side)])
    odd = (lax.axis_index("ctx") & 1) == 1
    grad_gain = jnp.concatenate(
        [jnp.where(odd, other_half, gain_half), jnp.where(odd, gain_half, other_half)], axis=1
    )
    (sent,) = call(
        corr_kernel,
        (f32(4 * side, side),),
        got,
        spectra,
        *tables,
        twist,
    )
    got = swap(sent, 4)
    grad_key, grad_value, grad_filter = call(
        last_outputs_kernel,
        (bf16(side, wide), bf16(side, wide), f32(side, wide)),
        got,
        key_proj,
        value_proj,
    )
    return (output, grad_query, grad_key, grad_value, grad_filter, grad_gain.reshape(wide))


def solution(mesh):
    both = P("ctx", "tp")
    return jax.shard_map(
        per_device,
        mesh=mesh,
        in_specs=(both, both, both, both, P("tp"), both),
        out_specs=(both, both, both, both, both, P("tp")),
        check_vma=False,
    )
```

time: 145 us -> 133 us (0.917)
  starting transfers between devices: 15.4 us -> 60.4 us
  blocking collectives: 77.2 us -> 32.7 us
  waiting for transfers between devices: 41 us -> 29 us
  local copies, waits for them, and re-layouts: 2.72 us -> 0.71 us
  Pallas kernels: 6.06 us -> 8.02 us
    all_to_all x2 -> x1, blocking collectives: 72.2 us -> 27.6 us  [swap(): lax.all_to_all(sent.reshape(shape), 'ctx', split_axis=0, concat_axis=0, a...]
    all_to_all x2 -> x3, starting transfers between devices: 15.4 us -> 58.5 us  [swap(): lax.all_to_all(sent.reshape(shape), 'ctx', split_axis=0, concat_axis=0, a...]
    all_to_all x2 -> x3, waiting for transfers between devices: 41 us -> 25.5 us  [swap(): lax.all_to_all(sent.reshape(shape), 'ctx', split_axis=0, concat_axis=0, a...]
    ppermute x0 -> x1, waiting for transfers between devices: none -> 3.5 us  [per_device(): lax.ppermute(gain_half, 'ctx', [(i, i ^ 1) for i in range(side)])]
    pallas_call x8 -> x9, Pallas kernels: 6.06 us -> 8.02 us  [call(): pl.pallas_call(kernel, out_shape=outs, compiler_params=pltpu.CompilerPara...]
    unnamed x26 -> x20, local copies, waits for them, and re-layouts: 2.63 us -> 0.71 us
    ppermute x0 -> x1, starting transfers between devices: none -> 1.91 us  [per_device(): lax.ppermute(gain_half, 'ctx', [(i, i ^ 1) for i in range(side)])]
  transfers between devices with their start and end apart: 2 -> 4, of which waited for: 2 -> 4; matrix products, arithmetic and copies ran while one was open for 0% -> 0% of each run, Pallas kernels for 1% -> 1%
where the time goes in v2:
time: 133 us; the launch traced here: 132 us
  starting transfers between devices  60.4 us (45%)
  blocking collectives  32.7 us (25%)
  waiting for transfers between devices  29 us (22%)
  Pallas kernels  8.02 us (6%)
    all_to_all x3, starting transfers between devices, swap(): lax.all_to_all(sent.reshape(shape), 'ctx', split_axis=0, concat_axis=0, a...  58.5 us
    all_to_all x1, blocking collectives, swap(): lax.all_to_all(sent.reshape(shape), 'ctx', split_axis=0, concat_axis=0, a...  27.6 us
    all_to_all x3, waiting for transfers between devices, swap(): lax.all_to_all(sent.reshape(shape), 'ctx', split_axis=0, concat_axis=0, a...  25.5 us
    pallas_call x9, Pallas kernels, call(): pl.pallas_call(kernel, out_shape=outs, compiler_params=pltpu.CompilerPara...  8.02 us
    all_gather x1, blocking collectives, per_device(): sums = lax.all_gather(sums, 'tp')  5.07 us
    ppermute x1, waiting for transfers between devices, per_device(): lax.ppermute(gain_half, 'ctx', [(i, i ^ 1) for i in range(side)])  3.5 us
  transfers between devices with their start and end apart: 4, of which 4 were waited for; matrix products, arithmetic and copies ran while one was open for 0% of the time, Pallas kernels for 1%

profile of v2, /device:TPU:24, one launch (start us, length us, event | category | flops | bytes accessed | tf_op | source)
XLA Modules:
  0.0 132.3 jit_solution(14925852884703025743)
XLA Ops:
  0.6 0.0 copy-start.5
  0.6 0.0 copy-start.6
  0.7 1.9 %shard_map.154 = f32[512,128]{1,0:T(8,128)} custom-call(bf16[128,256]{1,0:T(8,128)(2,1)} %key_ref.1, bf16[128,256]{1,0:T(8,128)(2,1)} %value_ref.1, f32[128,256]{1,0:T(8,128)} %filt_hbm.1), custom_call_target="tpu_custom_call" | custom-call | bytes 524288 | tf_op jit(solution)/shard_map/pallas_call | solution.py:246
  2.5 0.0 copy-start.1
  2.5 0.0 copy-start.2
  2.6 24.4 %all-to-all-start = ((f32[128,4,128]{2,1,0:T(4,128)}), f32[128,4,128]{2,1,0:T(4,128)S(1)}, u32[]{:S(2)}, u32[]{:S(2)}) async-start(f32[128,4,128]{2,1,0:T(4,128)} %bitcast.22), calls=%async_computation | async-start | bytes 524288 | tf_op jit(solution)/shard_map/all_to_all | solution.py:266
  27.0 0.0 copy-done.5
  27.0 0.0 copy-done.6
  27.0 0.0 copy-done.1
  27.0 0.0 copy-done.2
  27.0 0.0 copy-start
  27.0 0.1 shard_map.155
  27.2 13.2 %all-to-all-done = f32[128,4,128]{2,1,0:T(4,128)S(1)} async-done(((f32[128,4,128]{2,1,0:T(4,128)}), f32[128,4,128]{2,1,0:T(4,128)S(1)}, u32[]{:S(2)}, u32[]{:S(2)}) %all-to-all-start) | async-done | bytes 262176 | tf_op jit(solution)/shard_map/all_to_all | solution.py:266
  40.4 0.0 copy-done
  40.4 2.0 %shard_map.156 = (f32[256,128]{1,0:T(8,128)}, f32[4,2,128,128]{3,2,1,0:T(8,128)S(1)}) custom-call(f32[512,128]{1,0:T(8,128)S(1)} %bitcast.17, bf16[256,128]{1,0:T(8,128)(2,1)S(1)} %get-tuple-element.25.refs_0_, bf16[256,128]{1,0:T(8,128)(2,1)S(1)} %get-tuple-element.26.refs_1_, bf16[256,256]{1,0:T(8,128)(2,1)S(1)} %get-tuple-element.27.refs_2_, ...), custom_call_target="tpu_custom_call" | custom-call | bytes 1835008 | tf_op jit(solution)/shard_map/pallas_call | solution.py:246
  42.4 0.0 copy-start.7
  42.4 0.0 copy-start.8
  42.4 17.2 %all-to-all-start.1 = ((f32[128,2,128]{2,1,0:T(2,128)}), f32[128,2,128]{2,1,0:T(2,128)S(1)}, u32[]{:S(2)}, u32[]{:S(2)}) async-start(f32[128,2,128]{2,1,0:T(2,128)} %bitcast.2), calls=%async_computation.1 | async-start | bytes 262144 | tf_op jit(solution)/shard_map/all_to_all | solution.py:266
  59.6 0.0 copy-start.9
  59.6 0.0 copy-done.7
  59.6 0.0 copy-done.8
  59.6 0.7 copy-done.9
  60.2 0.1 shard_map.157
  60.4 6.3 %all-to-all-done.1 = f32[128,2,128]{2,1,0:T(2,128)S(1)} async-done(((f32[128,2,128]{2,1,0:T(2,128)}), f32[128,2,128]{2,1,0:T(2,128)S(1)}, u32[]{:S(2)}, u32[]{:S(2)}) %all-to-all-start.1) | async-done | bytes 131104 | tf_op jit(solution)/shard_map/all_to_all | solution.py:266
  66.7 5.1 %all-gather.1.sums_ref = f32[4,2,128]{2,1,0:T(2,128)S(1)} all-gather(f32[1,2,128]{2,1,0:T(2,128)S(1)} %bitcast.21), channel_id=2, replica_groups=mesh['ctx'=128,'tp'=4] {'tp'}, dimensions={0}, use_global_device_ids=true | all-gather | bytes 5120 | tf_op jit(solution)/shard_map/all_gather | solution.py:314
  71.8 0.2 shard_map.159
  72.0 27.6 %all_to_all.20 = f32[128,1,384]{2,1,0:T(1,128)S(1)} all-to-all(f32[128,1,384]{2,1,0:T(1,128)S(1)} %bitcast.18), channel_id=1, replica_groups={{392,136,396,140,384,128,388,132,408,152,412,156,400,144,404,148,424,16..., dimensions={0} | all-to-all | bytes 393216 | tf_op jit(solution)/shard_map/all_to_all | solution.py:266
  99.7 2.0 %shard_map.161 = f32[512,128]{1,0:T(8,128)} custom-call(f32[384,128]{1,0:T(8,128)S(1)} %bitcast.14, f32[4,2,128,128]{3,2,1,0:T(8,128)S(1)} %get-tuple-element.39.spec_ref, bf16[256,128]{1,0:T(8,128)(2,1)S(1)} %get-tuple-element.25.refs_0_, bf16[256,128]{1,0:T(8,128)(2,1)S(1)} %get-tuple-element.26.refs_1_, bf16[256,256]{1,0:T(8,128)(2,1)S(1)} %get-tuple-element.27.refs_2_, ...), custom_call_target="tpu_custom_call" | custom-call | bytes 1900544 | tf_op jit(solution)/shard_map/pallas_call | solution.py:246
  101.7 16.9 %all-to-all-start.3 = ((f32[128,4,128]{2,1,0:T(4,128)}), f32[128,4,128]{2,1,0:T(4,128)S(1)}, u32[]{:S(2)}, u32[]{:S(2)}) async-start(f32[128,4,128]{2,1,0:T(4,128)} %bitcast.8), calls=%async_computation.3 | async-start | bytes 524288 | tf_op jit(solution)/shard_map/all_to_all | solution.py:266
  118.6 0.0 copy-start.3
  118.6 0.0 copy-start.4
  118.7 0.8 shard_map.160
  119.4 1.9 %collective-permute-start = (f32[1,128]{1,0:T(1,128)S(1)}, f32[1,128]{1,0:T(1,128)S(1)}, u32[]{:S(2)}, u32[]{:S(2)}) collective-permute-start(f32[1,128]{1,0:T(1,128)S(1)} %get-tuple-element.43), channel_id=1, source_target_pairs={{0,4},{4,0},{8,12},{12,8},{16,20},{20,16},{24,28},{28,24},{32,36},... | collective-permute-start | bytes 1544 | tf_op jit(solution)/shard_map/ppermute | solution.py:327
  121.4 3.5 %collective-permute-done = f32[1,128]{1,0:T(1,128)S(1)} collective-permute-done((f32[1,128]{1,0:T(1,128)S(1)}, f32[1,128]{1,0:T(1,128)S(1)}, u32[]{:S(2)}, u32[]{:S(2)}) %collective-permute-start) | collective-permute-done | bytes 544 | tf_op jit(solution)/shard_map/ppermute | solution.py:327
  124.9 0.6 pad_maximum_fusion
  125.4 6.0 %all-to-all-done.3 = f32[128,4,128]{2,1,0:T(4,128)S(1)} async-done(((f32[128,4,128]{2,1,0:T(4,128)}), f32[128,4,128]{2,1,0:T(4,128)S(1)}, u32[]{:S(2)}, u32[]{:S(2)}) %all-to-all-start.3) | async-done | bytes 262176 | tf_op jit(solution)/shard_map/all_to_all | solution.py:266
  131.4 0.0 copy-done.3
  131.4 0.0 copy-done.4
  131.5 0.8 shard_map.162
  (2 shorter events, 0.0 us)
Async XLA Ops:
  0.6 26.4 %copy-start.5 = (f32[256,128]{1,0:T(8,128)S(1)}, f32[256,128]{1,0:T(8,128)}, u32[]{:S(2)}) copy-start(f32[256,128]{1,0:T(8,128)} %constant.18.clone.refs_0_) | copy-start | bytes 393220
  0.6 26.4 %copy-start.6 = (f32[128,256]{1,0:T(8,128)S(1)}, f32[128,256]{1,0:T(8,128)}, u32[]{:S(2)}) copy-start(f32[128,256]{1,0:T(8,128)} %constant.21.clone.refs_3_) | copy-start | bytes 393220
  2.5 24.5 %copy-start.1 = (f32[256,256]{1,0:T(8,128)S(1)}, f32[256,256]{1,0:T(8,128)}, u32[]{:S(2)}) copy-start(f32[256,256]{1,0:T(8,128)} %constant.19.clone.refs_1_) | copy-start | bytes 786436
  2.5 24.5 %copy-start.2 = (f32[256,256]{1,0:T(8,128)S(1)}, f32[256,256]{1,0:T(8,128)}, u32[]{:S(2)}) copy-start(f32[256,256]{1,0:T(8,128)} %constant.20.clone.refs_2_) | copy-start | bytes 786436
  2.6 37.8 %all-to-all-start = ((f32[128,4,128]{2,1,0:T(4,128)}), f32[128,4,128]{2,1,0:T(4,128)S(1)}, u32[]{:S(2)}, u32[]{:S(2)}) async-start(f32[128,4,128]{2,1,0:T(4,128)} %bitcast.22), calls=%async_computation | async-start | bytes 524288 | tf_op jit(solution)/shard_map/all_to_all | solution.py:266
  27.0 13.4 %copy-start = (f32[2,128,128]{2,1,0:T(8,128)S(1)}, f32[2,128,128]{2,1,0:T(8,128)}, u32[]{:S(2)}) copy-start(f32[2,128,128]{2,1,0:T(8,128)} %constant.22.clone.refs_8_) | copy-start | bytes 393220
  42.4 17.2 %copy-start.7 = (bf16[128,256]{1,0:T(8,128)(2,1)S(1)}, bf16[128,256]{1,0:T(8,128)(2,1)}, u32[]{:S(2)}) copy-start(bf16[128,256]{1,0:T(8,128)(2,1)} %query_ref.1) | copy-start | bytes 196612
  42.4 17.2 %copy-start.8 = (bf16[128,256]{1,0:T(8,128)(2,1)S(1)}, bf16[128,256]{1,0:T(8,128)(2,1)}, u32[]{:S(2)}) copy-start(bf16[128,256]{1,0:T(8,128)(2,1)} %cot_ref.1) | copy-start | bytes 196612
  42.4 24.3 %all-to-all-start.1 = ((f32[128,2,128]{2,1,0:T(2,128)}), f32[128,2,128]{2,1,0:T(2,128)S(1)}, u32[]{:S(2)}, u32[]{:S(2)}) async-start(f32[128,2,128]{2,1,0:T(2,128)} %bitcast.2), calls=%async_computation.1 | async-start | bytes 262144 | tf_op jit(solution)/shard_map/all_to_all | solution.py:266
  59.6 0.7 copy-start.9
  101.7 29.8 %all-to-all-start.3 = ((f32[128,4,128]{2,1,0:T(4,128)}), f32[128,4,128]{2,1,0:T(4,128)S(1)}, u32[]{:S(2)}, u32[]{:S(2)}) async-start(f32[128,4,128]{2,1,0:T(4,128)} %bitcast.8), calls=%async_computation.3 | async-start | bytes 524288 | tf_op jit(solution)/shard_map/all_to_all | solution.py:266
  118.6 12.8 %copy-start.3 = (bf16[128,256]{1,0:T(8,128)(2,1)S(1)}, bf16[128,256]{1,0:T(8,128)(2,1)}, u32[]{:S(2)}) copy-start(bf16[128,256]{1,0:T(8,128)(2,1)} %key_ref.1) | copy-start | bytes 196612
  118.6 12.8 %copy-start.4 = (bf16[128,256]{1,0:T(8,128)(2,1)S(1)}, bf16[128,256]{1,0:T(8,128)(2,1)}, u32[]{:S(2)}) copy-start(bf16[128,256]{1,0:T(8,128)(2,1)} %value_ref.1) | copy-start | bytes 196612
  119.4 5.4 %collective-permute-start = (f32[1,128]{1,0:T(1,128)S(1)}, f32[1,128]{1,0:T(1,128)S(1)}, u32[]{:S(2)}, u32[]{:S(2)}) collective-permute-start(f32[1,128]{1,0:T(1,128)S(1)} %get-tuple-element.43), channel_id=1, source_target_pairs={{0,4},{4,0},{8,12},{12,8},{16,20},{20,16},{24,28},{28,24},{32,36},... | collective-permute-start | bytes 1544 | tf_op jit(solution)/shard_map/ppermute | solution.py:327

commit v3 on v2

--- a/solution.py
+++ b/solution.py
@@ -48,26 +48,17 @@
     return jnp.dot(left, right, preferred_element_type=jnp.float32)
 
 
-def split_kernel(*refs):
-    count = len(refs) // 3
-    for i in range(count):
-        high, low = halves(refs[i][...])
-        refs[count + 2 * i][...] = high
-        refs[count + 2 * i + 1][...] = low
-
-
 def exact_dot(left, right):
     (left_high, left_low), (right_high, right_low) = left, right
     return dot(left_high, right_high) + (dot(left_high, right_low) + dot(left_low, right_high))
 
 
-def load(pair):
-    return pair[0][...], pair[1][...]
-
-
-def forward_spectra(columns, first, ahead, twist_ref):
+def forward_spectra(columns, first_ref, ahead_ref, twist_ref):
     count = len(columns)
-    mid = exact_dot(load(first), halves(jnp.concatenate(columns, axis=1)))
+    high, low = halves(jnp.concatenate(columns, axis=1))
+    first_high, first_low = halves(first_ref[...])
+    mid = dot(jnp.concatenate([first_high, first_high], axis=1), jnp.concatenate([high, low], axis=0))
+    mid = mid + dot(first_low, high)
     cos_t, sin_t = twist_ref[0], twist_ref[1]
     rows = []
     for u in range(count):
@@ -76,17 +67,17 @@
         rows.append(
             jnp.concatenate([real * cos_t - imag * sin_t, real * sin_t + imag * cos_t], axis=1)
         )
-    out = exact_dot(halves(jnp.concatenate(rows, axis=0)), load(ahead))
+    out = exact_dot(halves(jnp.concatenate(rows, axis=0)), halves(ahead_ref[...]))
     return [
         (out[u * side : (u + 1) * side, :side], out[u * side : (u + 1) * side, side:])
         for u in range(count)
     ]
 
 
-def inverse_columns(spectra, back, last, twist_ref):
+def inverse_columns(spectra, back_ref, last_ref, twist_ref):
     count = len(spectra)
     stacked = jnp.concatenate([jnp.concatenate(pair, axis=1) for pair in spectra], axis=0)
-    mid = exact_dot(halves(stacked), load(back))
+    mid = exact_dot(halves(stacked), halves(back_ref[...]))
     cos_t, sin_t = twist_ref[0], twist_ref[1]
     cols = []
     for u in range(count):
@@ -95,7 +86,7 @@
         cols.append(
             jnp.concatenate([real * cos_t + imag * sin_t, imag * cos_t - real * sin_t], axis=0)
         )
-    return exact_dot(load(last), halves(jnp.concatenate(cols, axis=1)))
+    return exact_dot(halves(last_ref[...]), halves(jnp.concatenate(cols, axis=1)))
 
 
 def product(left, right):
@@ -110,42 +101,42 @@
     return pl.ds(start, side, stride=stride)
 
 
-def send_inputs_kernel(key_hbm, value_hbm, filt_hbm, out_ref, key_ref, value_ref, filt_ref, sems):
-    pairs = ((key_hbm, key_ref), (value_hbm, value_ref), (filt_hbm, filt_ref))
-    copies = [pltpu.make_async_copy(a, b, sems.at[i]) for i, (a, b) in enumerate(pairs)]
+def first_kernel(key_hbm, value_hbm, filt_hbm, query_hbm, cot_hbm, gain_hbm, *refs):
+    sent_ref, query_t_ref, cot_t_ref, scaled_t_ref = refs[:4]
+    key_ref, value_ref, filt_ref, query_ref, cot_ref, gain_ref, sems = refs[4:]
+    sources = (filt_hbm, key_hbm, value_hbm, query_hbm, cot_hbm, gain_hbm)
+    targets = (filt_ref, key_ref, value_ref, query_ref, cot_ref, gain_ref)
+    copies = [
+        pltpu.make_async_copy(a, b, sems.at[i]) for i, (a, b) in enumerate(zip(sources, targets))
+    ]
     for copy in copies:
         copy.start()
-    for copy in copies:
+    halves_of = [slice(h * side, (h + 1) * side) for h in range(2)]
+    copies[0].wait()
+    for h, cols in enumerate(halves_of):
+        sent_ref[every(h, 4), :] = filt_ref[:, cols].T
+    copies[1].wait()
+    copies[2].wait()
+    for h, cols in enumerate(halves_of):
+        mixed = key_ref[:, cols].astype(jnp.float32) * value_ref[:, cols].astype(jnp.float32)
+        sent_ref[every(2 + h, 4), :] = mixed.T
+    for copy in copies[3:]:
         copy.wait()
-    mixed = key_ref[...].astype(jnp.float32) * value_ref[...].astype(jnp.float32)
-    filt = filt_ref[...]
-    for h in range(2):
-        cols = slice(h * side, (h + 1) * side)
-        out_ref[every(h, 4), :] = filt[:, cols].T
-        out_ref[every(2 + h, 4), :] = mixed[:, cols].T
-
-
-def flip_gates_kernel(query_ref, cot_ref, gain_ref, query_t_ref, cot_t_ref, scaled_t_ref):
-    query = query_ref[...].astype(jnp.float32)
-    cot = cot_ref[...].astype(jnp.float32)
-    scaled = cot * gain_ref[...]
-    for h in range(2):
-        cols = slice(h * side, (h + 1) * side)
-        query_t_ref[cols, :] = query[:, cols].T
-        cot_t_ref[cols, :] = cot[:, cols].T
-        scaled_t_ref[cols, :] = scaled[:, cols].T
-
-
-def conv_kernel(got_ref, *refs):
-    first, ahead, back, last = (refs[i : i + 2] for i in range(0, 8, 2))
-    twist_ref, out_ref, spec_ref = refs[8:]
+    for h, cols in enumerate(halves_of):
+        cot = cot_ref[:, cols].astype(jnp.float32)
+        query_t_ref[cols, :] = query_ref[:, cols].astype(jnp.float32).T
+        cot_t_ref[cols, :] = cot.T
+        scaled_t_ref[cols, :] = (cot * gain_ref[:, cols]).T
+
+
+def conv_kernel(got_ref, first_ref, ahead_ref, back_ref, last_ref, twist_ref, out_ref, spec_ref):
     columns = [got_ref[every(u, 4), :] for u in range(4)]
-    spectra = forward_spectra(columns, first, ahead, twist_ref)
+    spectra = forward_spectra(columns, first_ref, ahead_ref, twist_ref)
     for u in range(4):
         spec_ref[u, 0] = spectra[u][0]
         spec_ref[u, 1] = spectra[u][1]
     both = [product(spectra[h], spectra[2 + h]) for h in range(2)]
-    conv = inverse_columns(both, back, last, twist_ref)
+    conv = inverse_columns(both, back_ref, last_ref, twist_ref)
     for h in range(2):
         out_ref[every(h, 2), :] = conv[:, h * side : (h + 1) * side]
 
@@ -214,15 +205,15 @@
     gain_half_ref[...] = jnp.sum(got_ref[every(2, 3), :], axis=0, keepdims=True)
 
 
-def corr_kernel(got_ref, spec_ref, *refs):
-    first, ahead, back, last = (refs[i : i + 2] for i in range(0, 8, 2))
-    twist_ref, out_ref = refs[8:]
+def corr_kernel(
+    got_ref, spec_ref, first_ref, ahead_ref, back_ref, last_ref, twist_ref, out_ref
+):
     columns = [got_ref[every(h, 3), :] for h in range(2)]
-    spectra = forward_spectra(columns, first, ahead, twist_ref)
+    spectra = forward_spectra(columns, first_ref, ahead_ref, twist_ref)
     pairs = [
         conj_product((spec_ref[u, 0], spec_ref[u, 1]), spectra[u % 2]) for u in range(4)
     ]
-    result = inverse_columns(pairs, back, last, twist_ref)
+    result = inverse_columns(pairs, back_ref, last_ref, twist_ref)
     for u in range(4):
         out_ref[every(u, 4), :] = result[:, u * side : (u + 1) * side]
 
@@ -240,13 +231,13 @@
         grad_filter_ref[:, cols] = got_ref[every(2 + h, 4), :].T
 
 
-def call(kernel, outs, *operands, limit=vmem_bytes, **options):
+def call(kernel, outs, *operands, **options):
     moved = sum(math.prod(o.shape) * o.dtype.itemsize for o in operands)
     moved += sum(math.prod(o.shape) * o.dtype.itemsize for o in outs)
     result = pl.pallas_call(
         kernel,
         out_shape=outs,
-        compiler_params=pltpu.CompilerParams(vmem_limit_bytes=limit),
+        compiler_params=pltpu.CompilerParams(vmem_limit_bytes=vmem_bytes),
         cost_estimate=pl.CostEstimate(flops=0, bytes_accessed=moved, transcendentals=0),
         **options,
     )(*operands)
@@ -280,34 +271,25 @@
     gain = out_gain.reshape(1, wide)
 
     in_hbm = pl.BlockSpec(memory_space=pltpu.HBM)
-    (sent,) = call(
-        send_inputs_kernel,
-        (f32(4 * side, side),),
-        key_proj,
-        value_proj,
-        long_filter,
-        limit=None,
-        in_specs=[in_hbm] * 3,
+    inputs = (key_proj, value_proj, long_filter, gate_query, cotangent, gain)
+    sent, query_t, cot_t, scaled_t = call(
+        first_kernel,
+        (f32(4 * side, side),) + (f32(wide, side),) * 3,
+        *(pltpu.with_memory_space_constraint(x, pltpu.HBM) for x in inputs),
+        in_specs=[in_hbm] * 6,
         scratch_shapes=[
             pltpu.VMEM((side, wide), jnp.bfloat16),
             pltpu.VMEM((side, wide), jnp.bfloat16),
             pltpu.VMEM((side, wide), jnp.float32),
-            pltpu.SemaphoreType.DMA((3,)),
+            pltpu.VMEM((side, wide), jnp.bfloat16),
+            pltpu.VMEM((side, wide), jnp.bfloat16),
+            pltpu.VMEM((1, wide), jnp.float32),
+            pltpu.SemaphoreType.DMA((6,)),
         ],
     )
     got = swap(sent, 4)
-    tables = call(
-        split_kernel, tuple(bf16(*t.shape) for t in tables for _ in range(2)), *tables
-    )
-    query_t, cot_t, scaled_t = call(
-        flip_gates_kernel, (f32(wide, side),) * 3, gate_query, cotangent, gain
-    )
     sent, spectra = call(
-        conv_kernel,
-        (f32(wide, side), f32(4, 2, side, side)),
-        got,
-        *tables,
-        twist,
+        conv_kernel, (f32(wide, side), f32(4, 2, side, side)), got, *tables, twist
     )
     conv_t = swap(sent, 2)
     (sums,) = call(row_sums_kernel, (f32(2, side),), conv_t, query_t, scaled_t)

time: 133 us -> 131 us (0.985)
  blocking collectives: 32.7 us -> 94.2 us
  starting transfers between devices: 60.4 us -> 19 us
  waiting for transfers between devices: 29 us -> 9.5 us
  Pallas kernels: 8.02 us -> 6.51 us
    all_to_all x1 -> x3, blocking collectives: 27.6 us -> 89.2 us  [swap(): lax.all_to_all(sent.reshape(shape), 'ctx', split_axis=0, concat_axis=0, a...]
    all_to_all x3 -> x1, starting transfers between devices: 58.5 us -> 17.1 us  [swap(): lax.all_to_all(sent.reshape(shape), 'ctx', split_axis=0, concat_axis=0, a...]
    all_to_all x3 -> x1, waiting for transfers between devices: 25.5 us -> 5.99 us  [swap(): lax.all_to_all(sent.reshape(shape), 'ctx', split_axis=0, concat_axis=0, a...]
    pallas_call x9 -> x7, Pallas kernels: 8.02 us -> 6.51 us  [call(): pl.pallas_call(kernel, out_shape=outs, compiler_params=pltpu.CompilerPara...]
  transfers between devices with their start and end apart: 4 -> 2, of which waited for: 4 -> 2; matrix products, arithmetic and copies ran while one was open for 0% -> 0% of each run, Pallas kernels for 1% -> 1%
where the time goes in v3:
time: 131 us
  blocking collectives  94.2 us (72%)
  starting transfers between devices  19 us (15%)
  waiting for transfers between devices  9.5 us (7%)
  Pallas kernels  6.51 us (5%)
    all_to_all x3, blocking collectives, swap(): lax.all_to_all(sent.reshape(shape), 'ctx', split_axis=0, concat_axis=0, a...  89.2 us
    all_to_all x1, starting transfers between devices, swap(): lax.all_to_all(sent.reshape(shape), 'ctx', split_axis=0, concat_axis=0, a...  17.1 us
    pallas_call x7, Pallas kernels, call(): pl.pallas_call(kernel, out_shape=outs, compiler_params=pltpu.CompilerPara...  6.51 us
    all_to_all x1, waiting for transfers between devices, swap(): lax.all_to_all(sent.reshape(shape), 'ctx', split_axis=0, concat_axis=0, a...  5.99 us
    all_gather x1, blocking collectives, per_device(): sums = lax.all_gather(sums, 'tp')  5.07 us
    ppermute x1, waiting for transfers between devices, per_device(): lax.ppermute(gain_half, 'ctx', [(i, i ^ 1) for i in range(side)])  3.51 us
  transfers between devices with their start and end apart: 2, of which 2 were waited for; matrix products, arithmetic and copies ran while one was open for 0% of the time, Pallas kernels for 1%

profile of v3, /device:TPU:24, one launch (start us, length us, event | category | flops | bytes accessed | tf_op | source)
XLA Modules:
  0.0 130.6 jit_solution(423892891187792952)
XLA Ops:
  0.6 0.0 copy-start.2
  0.6 0.0 copy-start.3
  0.7 0.0 copy-start.4
  0.7 1.4 %shard_map.154 = (f32[512,128]{1,0:T(8,128)S(1)}, f32[256,128]{1,0:T(8,128)S(1)}, f32[256,128]{1,0:T(8,128)S(1)}, f32[256,128]{1,0:T(8,128)S(1)}) custom-call(bf16[128,256]{1,0:T(8,128)(2,1)} %key_ref.1, bf16[128,256]{1,0:T(8,128)(2,1)} %value_ref.1, f32[128,256]{1,0:T(8,128)} %filt_hbm.1, bf16[128,256]{1,0:T(8,128)(2,1)} %query_hbm.1, ...), custom_call_target="tpu_custom_call" | custom-call | bytes 1049600 | tf_op jit(solution)/shard_map/pallas_call | solution.py:237
  2.0 0.0 copy-start
  2.0 0.0 copy-start.1
  2.1 37.6 %all_to_all.20 = f32[128,4,128]{2,1,0:T(4,128)S(1)} all-to-all(f32[128,4,128]{2,1,0:T(4,128)S(1)} %bitcast.19), channel_id=1, replica_groups={{392,136,396,140,384,128,388,132,408,152,412,156,400,144,404,148,424,16..., dimensions={0} | all-to-all | bytes 524288 | tf_op jit(solution)/shard_map/all_to_all | solution.py:257
  39.7 0.0 copy-done.2
  39.7 0.0 copy-done.3
  39.7 0.0 copy-done.4
  39.7 0.0 copy-done
  39.7 0.0 copy-done.1
  39.7 1.3 shard_map.155
  41.0 23.9 %all_to_all.21 = f32[128,2,128]{2,1,0:T(2,128)S(1)} all-to-all(f32[128,2,128]{2,1,0:T(2,128)S(1)} %bitcast.20), channel_id=1, replica_groups={{392,136,396,140,384,128,388,132,408,152,412,156,400,144,404,148,424,16..., dimensions={0} | all-to-all | bytes 262144 | tf_op jit(solution)/shard_map/all_to_all | solution.py:257
  64.9 5.1 %all-gather.1.sums_ref = f32[4,2,128]{2,1,0:T(2,128)S(1)} all-gather(f32[1,2,128]{2,1,0:T(2,128)S(1)} %bitcast.23), channel_id=2, replica_groups=mesh['ctx'=128,'tp'=4] {'tp'}, dimensions={0}, use_global_device_ids=true | all-gather | bytes 5120 | tf_op jit(solution)/shard_map/all_gather | solution.py:296
  70.0 0.2 shard_map.157
  70.2 27.6 %all_to_all.22 = f32[128,1,384]{2,1,0:T(1,128)S(1)} all-to-all(f32[128,1,384]{2,1,0:T(1,128)S(1)} %bitcast.18), channel_id=1, replica_groups={{392,136,396,140,384,128,388,132,408,152,412,156,400,144,404,148,424,16..., dimensions={0} | all-to-all | bytes 393216 | tf_op jit(solution)/shard_map/all_to_all | solution.py:257
  97.9 2.0 %shard_map.159 = f32[512,128]{1,0:T(8,128)} custom-call(f32[384,128]{1,0:T(8,128)S(1)} %bitcast.14, f32[4,2,128,128]{3,2,1,0:T(8,128)S(1)} %get-tuple-element.25.spec_ref, f32[256,128]{1,0:T(8,128)S(1)} %copy-done.2, f32[256,256]{1,0:T(8,128)S(1)} %copy-done, f32[256,256]{1,0:T(8,128)S(1)} %copy-done.1, f32[128,256]{1,0:T(8,128)S(1)} %copy-done.3, ...), custom_call_target="tpu_custom_call" | custom-call | bytes 1900544 | tf_op jit(solution)/shard_map/pallas_call | solution.py:237
  99.9 0.0 copy-start.7
  99.9 17.1 %all-to-all-start.3 = ((f32[128,4,128]{2,1,0:T(4,128)}), f32[128,4,128]{2,1,0:T(4,128)S(1)}, u32[]{:S(2)}, u32[]{:S(2)}) async-start(f32[128,4,128]{2,1,0:T(4,128)} %bitcast.8), calls=%async_computation.3 | async-start | bytes 524288 | tf_op jit(solution)/shard_map/all_to_all | solution.py:257
  117.0 0.0 copy-done.7
  117.0 0.0 copy-start.5
  117.0 0.0 copy-start.6
  117.0 0.8 shard_map.158
  117.8 1.9 %collective-permute-start = (f32[1,128]{1,0:T(1,128)S(1)}, f32[1,128]{1,0:T(1,128)S(1)}, u32[]{:S(2)}, u32[]{:S(2)}) collective-permute-start(f32[1,128]{1,0:T(1,128)S(1)} %get-tuple-element.29), channel_id=1, source_target_pairs={{0,4},{4,0},{8,12},{12,8},{16,20},{20,16},{24,28},{28,24},{32,36},... | collective-permute-start | bytes 1544 | tf_op jit(solution)/shard_map/ppermute | solution.py:309
  119.7 3.5 %collective-permute-done = f32[1,128]{1,0:T(1,128)S(1)} collective-permute-done((f32[1,128]{1,0:T(1,128)S(1)}, f32[1,128]{1,0:T(1,128)S(1)}, u32[]{:S(2)}, u32[]{:S(2)}) %collective-permute-start) | collective-permute-done | bytes 544 | tf_op jit(solution)/shard_map/ppermute | solution.py:309
  123.2 0.6 pad_maximum_fusion
  123.8 6.0 %all-to-all-done.3 = f32[128,4,128]{2,1,0:T(4,128)S(1)} async-done(((f32[128,4,128]{2,1,0:T(4,128)}), f32[128,4,128]{2,1,0:T(4,128)S(1)}, u32[]{:S(2)}, u32[]{:S(2)}) %all-to-all-start.3) | async-done | bytes 262176 | tf_op jit(solution)/shard_map/all_to_all | solution.py:257
  129.8 0.0 copy-done.5
  129.8 0.0 copy-done.6
  129.8 0.8 shard_map.160
  (2 shorter events, 0.0 us)
Async XLA Ops:
  0.6 39.0 %copy-start.2 = (f32[256,128]{1,0:T(8,128)S(1)}, f32[256,128]{1,0:T(8,128)}, u32[]{:S(2)}) copy-start(f32[256,128]{1,0:T(8,128)} %constant.18.clone.first_ref) | copy-start | bytes 393220
  0.6 39.0 %copy-start.3 = (f32[128,256]{1,0:T(8,128)S(1)}, f32[128,256]{1,0:T(8,128)}, u32[]{:S(2)}) copy-start(f32[128,256]{1,0:T(8,128)} %constant.21.clone.last_ref) | copy-start | bytes 393220
  0.7 39.0 %copy-start.4 = (f32[2,128,128]{2,1,0:T(8,128)S(1)}, f32[2,128,128]{2,1,0:T(8,128)}, u32[]{:S(2)}) copy-start(f32[2,128,128]{2,1,0:T(8,128)} %constant.22.clone.twist_ref) | copy-start | bytes 393220
  2.0 37.6 %copy-start = (f32[256,256]{1,0:T(8,128)S(1)}, f32[256,256]{1,0:T(8,128)}, u32[]{:S(2)}) copy-start(f32[256,256]{1,0:T(8,128)} %constant.19.clone.ahead_ref) | copy-start | bytes 786436
  2.0 37.6 %copy-start.1 = (f32[256,256]{1,0:T(8,128)S(1)}, f32[256,256]{1,0:T(8,128)}, u32[]{:S(2)}) copy-start(f32[256,256]{1,0:T(8,128)} %constant.20.clone.back_ref) | copy-start | bytes 786436
  99.9 17.1 %copy-start.7 = (f32[256]{0:T(256)S(1)}, f32[256]{0:T(256)}, u32[]{:S(2)}) copy-start(f32[256]{0:T(256)} %param.15) | copy-start | bytes 3076
  99.9 29.9 %all-to-all-start.3 = ((f32[128,4,128]{2,1,0:T(4,128)}), f32[128,4,128]{2,1,0:T(4,128)S(1)}, u32[]{:S(2)}, u32[]{:S(2)}) async-start(f32[128,4,128]{2,1,0:T(4,128)} %bitcast.8), calls=%async_computation.3 | async-start | bytes 524288 | tf_op jit(solution)/shard_map/all_to_all | solution.py:257
  117.0 12.8 %copy-start.5 = (bf16[128,256]{1,0:T(8,128)(2,1)S(1)}, bf16[128,256]{1,0:T(8,128)(2,1)}, u32[]{:S(2)}) copy-start(bf16[128,256]{1,0:T(8,128)(2,1)} %key_ref.1) | copy-start | bytes 196612
  117.0 12.8 %copy-start.6 = (bf16[128,256]{1,0:T(8,128)(2,1)S(1)}, bf16[128,256]{1,0:T(8,128)(2,1)}, u32[]{:S(2)}) copy-start(bf16[128,256]{1,0:T(8,128)(2,1)} %value_ref.1) | copy-start | bytes 196612
  117.8 5.4 %collective-permute-start = (f32[1,128]{1,0:T(1,128)S(1)}, f32[1,128]{1,0:T(1,128)S(1)}, u32[]{:S(2)}, u32[]{:S(2)}) collective-permute-start(f32[1,128]{1,0:T(1,128)S(1)} %get-tuple-element.29), channel_id=1, source_target_pairs={{0,4},{4,0},{8,12},{12,8},{16,20},{20,16},{24,28},{28,24},{32,36},... | collective-permute-start | bytes 1544 | tf_op jit(solution)/shard_map/ppermute | solution.py:309

commit v4 on v3

--- a/solution.py
+++ b/solution.py
@@ -97,8 +97,8 @@
     return (left[0] * right[0] + left[1] * right[1], left[0] * right[1] - left[1] * right[0])
 
 
-def every(start, stride):
-    return pl.ds(start, side, stride=stride)
+def slice_of(u):
+    return slice(u * side, (u + 1) * side)
 
 
 def first_kernel(key_hbm, value_hbm, filt_hbm, query_hbm, cot_hbm, gain_hbm, *refs):
@@ -114,12 +114,12 @@
     halves_of = [slice(h * side, (h + 1) * side) for h in range(2)]
     copies[0].wait()
     for h, cols in enumerate(halves_of):
-        sent_ref[every(h, 4), :] = filt_ref[:, cols].T
+        sent_ref[:, h, :] = filt_ref[:, cols].T
     copies[1].wait()
     copies[2].wait()
     for h, cols in enumerate(halves_of):
         mixed = key_ref[:, cols].astype(jnp.float32) * value_ref[:, cols].astype(jnp.float32)
-        sent_ref[every(2 + h, 4), :] = mixed.T
+        sent_ref[:, 2 + h, :] = mixed.T
     for copy in copies[3:]:
         copy.wait()
     for h, cols in enumerate(halves_of):
@@ -130,7 +130,7 @@
 
 
 def conv_kernel(got_ref, first_ref, ahead_ref, back_ref, last_ref, twist_ref, out_ref, spec_ref):
-    columns = [got_ref[every(u, 4), :] for u in range(4)]
+    columns = [got_ref[:, u, :] for u in range(4)]
     spectra = forward_spectra(columns, first_ref, ahead_ref, twist_ref)
     for u in range(4):
         spec_ref[u, 0] = spectra[u][0]
@@ -138,7 +138,7 @@
     both = [product(spectra[h], spectra[2 + h]) for h in range(2)]
     conv = inverse_columns(both, back_ref, last_ref, twist_ref)
     for h in range(2):
-        out_ref[every(h, 2), :] = conv[:, h * side : (h + 1) * side]
+        out_ref[:, h, :] = conv[:, h * side : (h + 1) * side]
 
 
 def row_sums_kernel(conv_ref, query_t_ref, scaled_t_ref, out_ref):
@@ -146,7 +146,7 @@
     dots = jnp.zeros((1, side), jnp.float32)
     for h in range(2):
         cols = slice(h * side, (h + 1) * side)
-        gated = conv_ref[every(h, 2), :] * query_t_ref[cols, :]
+        gated = conv_ref[:, h, :] * query_t_ref[cols, :]
         squares = squares + jnp.sum(gated * gated, axis=0, keepdims=True)
         dots = dots + jnp.sum(scaled_t_ref[cols, :] * gated, axis=0, keepdims=True)
     out_ref[0:1, :] = squares
@@ -171,13 +171,13 @@
         cols = slice(h * side, (h + 1) * side)
         query = query_t_ref[cols, :]
         cot = cot_t_ref[cols, :]
-        gated = conv_ref[every(h, 2), :] * query
+        gated = conv_ref[:, h, :] * query
         scaled = scaled_t_ref[cols, :]
-        out_ref[every(h, 3), :] = (inv_rms * scaled - gated * pull) * query
+        out_ref[:, 0, slice_of(h)] = (inv_rms * scaled - gated * pull) * query
         part = jnp.sum(cot * gated * inv_rms, axis=1, keepdims=True)
         parts.append(jnp.broadcast_to(part, (side, side)).T)
     number = lax.broadcasted_iota(jnp.int32, (side, side), 0)
-    out_ref[every(2, 3), :] = jnp.where((number & 2) == 0, parts[0], parts[1])
+    out_ref[:, 0, slice_of(2)] = jnp.where((number & 2) == 0, parts[0], parts[1])
 
 
 def row_outputs_kernel(
@@ -195,27 +195,27 @@
     pull = inv_rms * inv_rms * inv_rms * row_dot
     for h in range(2):
         cols = slice(h * side, (h + 1) * side)
-        conv = conv_ref[every(h, 2), :]
+        conv = conv_ref[:, h, :]
         gated = conv * query_t_ref[cols, :]
         scaled = scaled_t_ref[cols, :]
         normed = (gated * inv_rms).T
         output_ref[:, cols] = (normed * gain_ref[:, cols]).astype(jnp.bfloat16)
         grad = (inv_rms * scaled - gated * pull) * conv
         grad_query_ref[:, cols] = grad.T.astype(jnp.bfloat16)
-    gain_half_ref[...] = jnp.sum(got_ref[every(2, 3), :], axis=0, keepdims=True)
+    gain_half_ref[...] = jnp.sum(got_ref[:, 0, slice_of(2)], axis=0, keepdims=True)
 
 
 def corr_kernel(
     got_ref, spec_ref, first_ref, ahead_ref, back_ref, last_ref, twist_ref, out_ref
 ):
-    columns = [got_ref[every(h, 3), :] for h in range(2)]
+    columns = [got_ref[:, 0, slice_of(h)] for h in range(2)]
     spectra = forward_spectra(columns, first_ref, ahead_ref, twist_ref)
     pairs = [
         conj_product((spec_ref[u, 0], spec_ref[u, 1]), spectra[u % 2]) for u in range(4)
     ]
     result = inverse_columns(pairs, back_ref, last_ref, twist_ref)
     for u in range(4):
-        out_ref[every(u, 4), :] = result[:, u * side : (u + 1) * side]
+        out_ref[:, u, :] = result[:, u * side : (u + 1) * side]
 
 
 def last_outputs_kernel(
@@ -223,12 +223,12 @@
 ):
     for h in range(2):
         cols = slice(h * side, (h + 1) * side)
-        d_mixed = got_ref[every(h, 4), :].T
+        d_mixed = got_ref[:, h, :].T
         value = value_ref[:, cols].astype(jnp.float32)
         key = key_ref[:, cols].astype(jnp.float32)
         grad_key_ref[:, cols] = (d_mixed * value).astype(jnp.bfloat16)
         grad_value_ref[:, cols] = (d_mixed * key).astype(jnp.bfloat16)
-        grad_filter_ref[:, cols] = got_ref[every(2 + h, 4), :].T
+        grad_filter_ref[:, cols] = got_ref[:, 2 + h, :].T
 
 
 def call(kernel, outs, *operands, **options):
@@ -252,17 +252,16 @@
     return jax.ShapeDtypeStruct(shape, jnp.bfloat16)
 
 
-def swap(sent, rows):
-    shape = (side, 1, rows * side) if rows == 3 else (side, rows, side)
+def swap(sent):
     got = lax.all_to_all(
-        sent.reshape(shape),
+        sent,
         "ctx",
         split_axis=0,
         concat_axis=0,
         axis_index_groups=[swap_order()],
         tiled=True,
     )
-    return got.reshape(side * rows, side)
+    return got
 
 
 def per_device(gate_query, key_proj, value_proj, long_filter, out_gain, cotangent):
@@ -274,7 +273,7 @@
     inputs = (key_proj, value_proj, long_filter, gate_query, cotangent, gain)
     sent, query_t, cot_t, scaled_t = call(
         first_kernel,
-        (f32(4 * side, side),) + (f32(wide, side),) * 3,
+        (f32(side, 4, side),) + (f32(wide, side),) * 3,
         *(pltpu.with_memory_space_constraint(x, pltpu.HBM) for x in inputs),
         in_specs=[in_hbm] * 6,
         scratch_shapes=[
@@ -287,15 +286,15 @@
             pltpu.SemaphoreType.DMA((6,)),
         ],
     )
-    got = swap(sent, 4)
+    got = swap(sent)
     sent, spectra = call(
-        conv_kernel, (f32(wide, side), f32(4, 2, side, side)), got, *tables, twist
-    )
-    conv_t = swap(sent, 2)
+        conv_kernel, (f32(side, 2, side), f32(4, 2, side, side)), got, *tables, twist
+    )
+    conv_t = swap(sent)
     (sums,) = call(row_sums_kernel, (f32(2, side),), conv_t, query_t, scaled_t)
     sums = lax.all_gather(sums, "tp")
-    (sent,) = call(d_conv_kernel, (f32(3 * side, side),), conv_t, query_t, cot_t, scaled_t, sums)
-    got = swap(sent, 3)
+    (sent,) = call(d_conv_kernel, (f32(side, 1, 3 * side),), conv_t, query_t, cot_t, scaled_t, sums)
+    got = swap(sent)
     output, grad_query, gain_half = call(
         row_outputs_kernel,
         (bf16(side, wide), bf16(side, wide), f32(1, side)),
@@ -313,13 +312,13 @@
     )
     (sent,) = call(
         corr_kernel,
-        (f32(4 * side, side),),
+        (f32(side, 4, side),),
         got,
         spectra,
         *tables,
         twist,
     )
-    got = swap(sent, 4)
+    got = swap(sent)
     grad_key, grad_value, grad_filter = call(
         last_outputs_kernel,
         (bf16(side, wide), bf16(side, wide), f32(side, wide)),

time: 131 us -> 132 us (level)
  no operation moved by 1% of the time
where the time goes in v4:
time: 132 us; the launch traced here: 131 us
  blocking collectives  94.2 us (71%)
  starting transfers between devices  19 us (14%)
  waiting for transfers between devices  9.46 us (7%)
  Pallas kernels  7.17 us (5%)
    all_to_all x3, blocking collectives, swap(): lax.all_to_all(sent, 'ctx', split_axis=0, concat_axis=0, axis_index_group...  89.2 us
    all_to_all x1, starting transfers between devices, swap(): lax.all_to_all(sent, 'ctx', split_axis=0, concat_axis=0, axis_index_group...  17.1 us
    pallas_call x7, Pallas kernels, call(): pl.pallas_call(kernel, out_shape=outs, compiler_params=pltpu.CompilerPara...  7.17 us
    all_to_all x1, waiting for transfers between devices, swap(): lax.all_to_all(sent, 'ctx', split_axis=0, concat_axis=0, axis_index_group...  5.96 us
    all_gather x1, blocking collectives, per_device(): sums = lax.all_gather(sums, 'tp')  5.07 us
    ppermute x1, waiting for transfers between devices, per_device(): lax.ppermute(gain_half, 'ctx', [(i, i ^ 1) for i in range(side)])  3.5 us
  transfers between devices with their start and end apart: 2, of which 2 were waited for; matrix products, arithmetic and copies ran while one was open for 0% of the time, Pallas kernels for 1%

profile of v4, /device:TPU:24, one launch (start us, length us, event | category | flops | bytes accessed | tf_op | source)
XLA Modules:
  0.0 131.2 jit_solution(14767451145180641435)
XLA Ops:
  0.6 0.0 copy-start.2
  0.6 0.0 copy-start.3
  0.7 0.0 copy-start.4
  0.7 1.4 %shard_map.154 = (f32[128,4,128]{2,1,0:T(4,128)S(1)}, f32[256,128]{1,0:T(8,128)S(1)}, f32[256,128]{1,0:T(8,128)S(1)}, f32[256,128]{1,0:T(8,128)S(1)}) custom-call(bf16[128,256]{1,0:T(8,128)(2,1)} %key_ref.1, bf16[128,256]{1,0:T(8,128)(2,1)} %value_ref.1, f32[128,256]{1,0:T(8,128)} %filt_hbm.1, bf16[128,256]{1,0:T(8,128)(2,1)} %query_hbm.1, ...), custom_call_target="tpu_custom_call" | custom-call | bytes 1049600 | tf_op jit(solution)/shard_map/pallas_call | solution.py:237
  2.1 0.0 copy-start
  2.1 0.0 copy-start.1
  2.1 37.6 %all_to_all.20.got_ref = f32[128,4,128]{2,1,0:T(4,128)S(1)} all-to-all(f32[128,4,128]{2,1,0:T(4,128)S(1)} %get-tuple-element.18), channel_id=1, replica_groups={{392,136,396,140,384,128,388,132,408,152,412,156,400,144,404,148,424,16..., dimensions={0} | all-to-all | bytes 524288 | tf_op jit(solution)/shard_map/all_to_all | solution.py:256
  39.8 0.0 copy-done.2
  39.8 0.0 copy-done.3
  39.8 0.0 copy-done.4
  39.8 0.0 copy-done
  39.8 0.0 copy-done.1
  39.8 1.4 %shard_map.155 = (f32[128,2,128]{2,1,0:T(2,128)S(1)}, f32[4,2,128,128]{3,2,1,0:T(8,128)S(1)}) custom-call(f32[128,4,128]{2,1,0:T(4,128)S(1)} %all_to_all.20.got_ref, f32[256,128]{1,0:T(8,128)S(1)} %copy-done.2, f32[256,256]{1,0:T(8,128)S(1)} %copy-done, f32[256,256]{1,0:T(8,128)S(1)} %copy-done.1, f32[128,256]{1,0:T(8,128)S(1)} %copy-done.3, ...), custom_call_target="tpu_custom_call" | custom-call | bytes 1835008 | tf_op jit(solution)/shard_map/pallas_call | solution.py:237
  41.2 23.9 %all_to_all.21.conv_ref = f32[128,2,128]{2,1,0:T(2,128)S(1)} all-to-all(f32[128,2,128]{2,1,0:T(2,128)S(1)} %get-tuple-element.19), channel_id=1, replica_groups={{392,136,396,140,384,128,388,132,408,152,412,156,400,144,404,148,424,16..., dimensions={0} | all-to-all | bytes 262144 | tf_op jit(solution)/shard_map/all_to_all | solution.py:256
  65.1 0.1 shard_map.156
  65.2 5.1 %all-gather.1.sums_ref = f32[4,2,128]{2,1,0:T(2,128)S(1)} all-gather(f32[1,2,128]{2,1,0:T(2,128)S(1)} %bitcast.5), channel_id=2, replica_groups=mesh['ctx'=128,'tp'=4] {'tp'}, dimensions={0}, use_global_device_ids=true | all-gather | bytes 5120 | tf_op jit(solution)/shard_map/all_gather | solution.py:295
  70.3 0.3 shard_map.157
  70.6 27.6 %all_to_all.22.got_ref = f32[128,1,384]{2,1,0:T(1,128)S(1)} all-to-all(f32[128,1,384]{2,1,0:T(1,128)S(1)} %shard_map.157), channel_id=1, replica_groups={{392,136,396,140,384,128,388,132,408,152,412,156,400,144,404,148,424,16..., dimensions={0} | all-to-all | bytes 393216 | tf_op jit(solution)/shard_map/all_to_all | solution.py:256
  98.3 2.2 %shard_map.159 = f32[128,4,128]{2,1,0:T(4,128)} custom-call(f32[128,1,384]{2,1,0:T(1,128)S(1)} %all_to_all.22.got_ref, f32[4,2,128,128]{3,2,1,0:T(8,128)S(1)} %get-tuple-element.25.spec_ref, f32[256,128]{1,0:T(8,128)S(1)} %copy-done.2, f32[256,256]{1,0:T(8,128)S(1)} %copy-done, f32[256,256]{1,0:T(8,128)S(1)} %copy-done.1, f32[128,256]{1,0:T(8,128)S(1)} %copy-done.3, ...), custom_call_target="tpu_custom_call" | custom-call | bytes 1900544 | tf_op jit(solution)/shard_map/pallas_call | solution.py:237
  100.4 0.0 copy-start.7
  100.4 17.1 %all-to-all-start.3 = ((f32[128,4,128]{2,1,0:T(4,128)}), f32[128,4,128]{2,1,0:T(4,128)S(1)}, u32[]{:S(2)}, u32[]{:S(2)}) async-start(f32[128,4,128]{2,1,0:T(4,128)} %shard_map.159), calls=%async_computation.3 | async-start | bytes 524288 | tf_op jit(solution)/shard_map/all_to_all | solution.py:256
  117.5 0.0 copy-done.7
  117.5 0.0 copy-start.5
  117.5 0.0 copy-start.6
  117.5 0.8 shard_map.158
  118.4 1.9 %collective-permute-start = (f32[1,128]{1,0:T(1,128)S(1)}, f32[1,128]{1,0:T(1,128)S(1)}, u32[]{:S(2)}, u32[]{:S(2)}) collective-permute-start(f32[1,128]{1,0:T(1,128)S(1)} %get-tuple-element.29), channel_id=1, source_target_pairs={{0,4},{4,0},{8,12},{12,8},{16,20},{20,16},{24,28},{28,24},{32,36},... | collective-permute-start | bytes 1544 | tf_op jit(solution)/shard_map/ppermute | solution.py:308
  120.3 3.5 %collective-permute-done = f32[1,128]{1,0:T(1,128)S(1)} collective-permute-done((f32[1,128]{1,0:T(1,128)S(1)}, f32[1,128]{1,0:T(1,128)S(1)}, u32[]{:S(2)}, u32[]{:S(2)}) %collective-permute-start) | collective-permute-done | bytes 544 | tf_op jit(solution)/shard_map/ppermute | solution.py:308
  123.8 0.6 pad_maximum_fusion
  124.4 6.0 %all-to-all-done.3.got_ref = f32[128,4,128]{2,1,0:T(4,128)S(1)} async-done(((f32[128,4,128]{2,1,0:T(4,128)}), f32[128,4,128]{2,1,0:T(4,128)S(1)}, u32[]{:S(2)}, u32[]{:S(2)}) %all-to-all-start.3) | async-done | bytes 262176 | tf_op jit(solution)/shard_map/all_to_all | solution.py:256
  130.3 0.0 copy-done.5
  130.3 0.0 copy-done.6
  130.3 0.9 shard_map.160
  (1 shorter events, 0.0 us)
Async XLA Ops:
  0.6 39.1 %copy-start.2 = (f32[256,128]{1,0:T(8,128)S(1)}, f32[256,128]{1,0:T(8,128)}, u32[]{:S(2)}) copy-start(f32[256,128]{1,0:T(8,128)} %constant.18.clone.first_ref) | copy-start | bytes 393220
  0.6 39.1 %copy-start.3 = (f32[128,256]{1,0:T(8,128)S(1)}, f32[128,256]{1,0:T(8,128)}, u32[]{:S(2)}) copy-start(f32[128,256]{1,0:T(8,128)} %constant.21.clone.last_ref) | copy-start | bytes 393220
  0.7 39.1 %copy-start.4 = (f32[2,128,128]{2,1,0:T(8,128)S(1)}, f32[2,128,128]{2,1,0:T(8,128)}, u32[]{:S(2)}) copy-start(f32[2,128,128]{2,1,0:T(8,128)} %constant.22.clone.twist_ref) | copy-start | bytes 393220
  2.1 37.6 %copy-start = (f32[256,256]{1,0:T(8,128)S(1)}, f32[256,256]{1,0:T(8,128)}, u32[]{:S(2)}) copy-start(f32[256,256]{1,0:T(8,128)} %constant.19.clone.ahead_ref) | copy-start | bytes 786436
  2.1 37.6 %copy-start.1 = (f32[256,256]{1,0:T(8,128)S(1)}, f32[256,256]{1,0:T(8,128)}, u32[]{:S(2)}) copy-start(f32[256,256]{1,0:T(8,128)} %constant.20.clone.back_ref) | copy-start | bytes 786436
  100.4 17.1 %copy-start.7 = (f32[256]{0:T(256)S(1)}, f32[256]{0:T(256)}, u32[]{:S(2)}) copy-start(f32[256]{0:T(256)} %param.15) | copy-start | bytes 3076
  100.4 29.9 %all-to-all-start.3 = ((f32[128,4,128]{2,1,0:T(4,128)}), f32[128,4,128]{2,1,0:T(4,128)S(1)}, u32[]{:S(2)}, u32[]{:S(2)}) async-start(f32[128,4,128]{2,1,0:T(4,128)} %shard_map.159), calls=%async_computation.3 | async-start | bytes 524288 | tf_op jit(solution)/shard_map/all_to_all | solution.py:256
  117.5 12.8 %copy-start.5 = (bf16[128,256]{1,0:T(8,128)(2,1)S(1)}, bf16[128,256]{1,0:T(8,128)(2,1)}, u32[]{:S(2)}) copy-start(bf16[128,256]{1,0:T(8,128)(2,1)} %key_ref.1) | copy-start | bytes 196612
  117.5 12.8 %copy-start.6 = (bf16[128,256]{1,0:T(8,128)(2,1)S(1)}, bf16[128,256]{1,0:T(8,128)(2,1)}, u32[]{:S(2)}) copy-start(bf16[128,256]{1,0:T(8,128)(2,1)} %value_ref.1) | copy-start | bytes 196612
  118.4 5.4 %collective-permute-start = (f32[1,128]{1,0:T(1,128)S(1)}, f32[1,128]{1,0:T(1,128)S(1)}, u32[]{:S(2)}, u32[]{:S(2)}) collective-permute-start(f32[1,128]{1,0:T(1,128)S(1)} %get-tuple-element.29), channel_id=1, source_target_pairs={{0,4},{4,0},{8,12},{12,8},{16,20},{20,16},{24,28},{28,24},{32,36},... | collective-permute-start | bytes 1544 | tf_op jit(solution)/shard_map/ppermute | solution.py:308

commit v5 on v4

--- a/solution.py
+++ b/solution.py
@@ -38,27 +38,15 @@
     return tuple(t.astype(np.float32) for t in (first, ahead, back, last)) + (twist,)
 
 
-def halves(value):
-    high = value.astype(jnp.bfloat16)
-    low = (value - high.astype(jnp.float32)).astype(jnp.bfloat16)
-    return high, low
-
-
-def dot(left, right):
-    return jnp.dot(left, right, preferred_element_type=jnp.float32)
-
-
 def exact_dot(left, right):
-    (left_high, left_low), (right_high, right_low) = left, right
-    return dot(left_high, right_high) + (dot(left_high, right_low) + dot(left_low, right_high))
+    return jnp.dot(
+        left, right, precision=lax.Precision.HIGHEST, preferred_element_type=jnp.float32
+    )
 
 
 def forward_spectra(columns, first_ref, ahead_ref, twist_ref):
     count = len(columns)
-    high, low = halves(jnp.concatenate(columns, axis=1))
-    first_high, first_low = halves(first_ref[...])
-    mid = dot(jnp.concatenate([first_high, first_high], axis=1), jnp.concatenate([high, low], axis=0))
-    mid = mid + dot(first_low, high)
+    mid = exact_dot(first_ref[...], jnp.concatenate(columns, axis=1))
     cos_t, sin_t = twist_ref[0], twist_ref[1]
     rows = []
     for u in range(count):
@@ -67,7 +55,7 @@
         rows.append(
             jnp.concatenate([real * cos_t - imag * sin_t, real * sin_t + imag * cos_t], axis=1)
         )
-    out = exact_dot(halves(jnp.concatenate(rows, axis=0)), halves(ahead_ref[...]))
+    out = exact_dot(jnp.concatenate(rows, axis=0), ahead_ref[...])
     return [
         (out[u * side : (u + 1) * side, :side], out[u * side : (u + 1) * side, side:])
         for u in range(count)
@@ -77,7 +65,7 @@
 def inverse_columns(spectra, back_ref, last_ref, twist_ref):
     count = len(spectra)
     stacked = jnp.concatenate([jnp.concatenate(pair, axis=1) for pair in spectra], axis=0)
-    mid = exact_dot(halves(stacked), halves(back_ref[...]))
+    mid = exact_dot(stacked, back_ref[...])
     cos_t, sin_t = twist_ref[0], twist_ref[1]
     cols = []
     for u in range(count):
@@ -86,7 +74,7 @@
         cols.append(
             jnp.concatenate([real * cos_t + imag * sin_t, imag * cos_t - real * sin_t], axis=0)
         )
-    return exact_dot(halves(last_ref[...]), halves(jnp.concatenate(cols, axis=1)))
+    return exact_dot(last_ref[...], jnp.concatenate(cols, axis=1))
 
 
 def product(left, right):

time: 132 us -> 134 us (1.015)
  Pallas kernels: 7.17 us -> 9.11 us
    pallas_call x7, Pallas kernels: 7.17 us -> 9.11 us  [call(): pl.pallas_call(kernel, out_shape=outs, compiler_params=pltpu.CompilerPara...]
where the time goes in v5:
time: 134 us; the launch traced here: 133 us
  blocking collectives  94.2 us (70%)
  starting transfers between devices  19 us (14%)
  waiting for transfers between devices  9.46 us (7%)
  Pallas kernels  9.11 us (7%)
    all_to_all x3, blocking collectives, swap(): lax.all_to_all(sent, 'ctx', split_axis=0, concat_axis=0, axis_index_group...  89.2 us
    all_to_all x1, starting transfers between devices, swap(): lax.all_to_all(sent, 'ctx', split_axis=0, concat_axis=0, axis_index_group...  17.1 us
    pallas_call x7, Pallas kernels, call(): pl.pallas_call(kernel, out_shape=outs, compiler_params=pltpu.CompilerPara...  9.11 us
    all_to_all x1, waiting for transfers between devices, swap(): lax.all_to_all(sent, 'ctx', split_axis=0, concat_axis=0, axis_index_group...  5.96 us
    all_gather x1, blocking collectives, per_device(): sums = lax.all_gather(sums, 'tp')  5.07 us
    ppermute x1, waiting for transfers between devices, per_device(): lax.ppermute(gain_half, 'ctx', [(i, i ^ 1) for i in range(side)])  3.5 us
  transfers between devices with their start and end apart: 2, of which 2 were waited for; matrix products, arithmetic and copies ran while one was open for 0% of the time, Pallas kernels for 1%

profile of v5, /device:TPU:24, one launch (start us, length us, event | category | flops | bytes accessed | tf_op | source)
XLA Modules:
  0.0 133.2 jit_solution(3923776218412385784)
XLA Ops:
  0.6 0.0 copy-start.2
  0.6 0.0 copy-start.3
  0.7 0.0 copy-start.4
  0.7 1.4 %shard_map.154 = (f32[128,4,128]{2,1,0:T(4,128)S(1)}, f32[256,128]{1,0:T(8,128)S(1)}, f32[256,128]{1,0:T(8,128)S(1)}, f32[256,128]{1,0:T(8,128)S(1)}) custom-call(bf16[128,256]{1,0:T(8,128)(2,1)} %key_ref.1, bf16[128,256]{1,0:T(8,128)(2,1)} %value_ref.1, f32[128,256]{1,0:T(8,128)} %filt_hbm.1, bf16[128,256]{1,0:T(8,128)(2,1)} %query_hbm.1, ...), custom_call_target="tpu_custom_call" | custom-call | bytes 1049600 | tf_op jit(solution)/shard_map/pallas_call | solution.py:225
  2.1 0.0 copy-start
  2.1 0.0 copy-start.1
  2.1 37.6 %all_to_all.20.got_ref = f32[128,4,128]{2,1,0:T(4,128)S(1)} all-to-all(f32[128,4,128]{2,1,0:T(4,128)S(1)} %get-tuple-element.18), channel_id=1, replica_groups={{392,136,396,140,384,128,388,132,408,152,412,156,400,144,404,148,424,16..., dimensions={0} | all-to-all | bytes 524288 | tf_op jit(solution)/shard_map/all_to_all | solution.py:244
  39.8 0.0 copy-done.2
  39.8 0.0 copy-done.3
  39.8 0.0 copy-done.4
  39.8 0.0 copy-done
  39.8 0.0 copy-done.1
  39.8 2.5 %shard_map.155 = (f32[128,2,128]{2,1,0:T(2,128)S(1)}, f32[4,2,128,128]{3,2,1,0:T(8,128)S(1)}) custom-call(f32[128,4,128]{2,1,0:T(4,128)S(1)} %all_to_all.20.got_ref, f32[256,128]{1,0:T(8,128)S(1)} %copy-done.2, f32[256,256]{1,0:T(8,128)S(1)} %copy-done, f32[256,256]{1,0:T(8,128)S(1)} %copy-done.1, f32[128,256]{1,0:T(8,128)S(1)} %copy-done.3, ...), custom_call_target="tpu_custom_call" | custom-call | bytes 1835008 | tf_op jit(solution)/shard_map/pallas_call | solution.py:225
  42.2 23.9 %all_to_all.21.conv_ref = f32[128,2,128]{2,1,0:T(2,128)S(1)} all-to-all(f32[128,2,128]{2,1,0:T(2,128)S(1)} %get-tuple-element.19), channel_id=1, replica_groups={{392,136,396,140,384,128,388,132,408,152,412,156,400,144,404,148,424,16..., dimensions={0} | all-to-all | bytes 262144 | tf_op jit(solution)/shard_map/all_to_all | solution.py:244
  66.2 0.1 shard_map.156
  66.3 5.1 %all-gather.1.sums_ref = f32[4,2,128]{2,1,0:T(2,128)S(1)} all-gather(f32[1,2,128]{2,1,0:T(2,128)S(1)} %bitcast.5), channel_id=2, replica_groups=mesh['ctx'=128,'tp'=4] {'tp'}, dimensions={0}, use_global_device_ids=true | all-gather | bytes 5120 | tf_op jit(solution)/shard_map/all_gather | solution.py:283
  71.3 0.3 shard_map.157
  71.6 27.6 %all_to_all.22.got_ref = f32[128,1,384]{2,1,0:T(1,128)S(1)} all-to-all(f32[128,1,384]{2,1,0:T(1,128)S(1)} %shard_map.157), channel_id=1, replica_groups={{392,136,396,140,384,128,388,132,408,152,412,156,400,144,404,148,424,16..., dimensions={0} | all-to-all | bytes 393216 | tf_op jit(solution)/shard_map/all_to_all | solution.py:244
  99.3 3.1 %shard_map.159 = f32[128,4,128]{2,1,0:T(4,128)} custom-call(f32[128,1,384]{2,1,0:T(1,128)S(1)} %all_to_all.22.got_ref, f32[4,2,128,128]{3,2,1,0:T(8,128)S(1)} %get-tuple-element.25.spec_ref, f32[256,128]{1,0:T(8,128)S(1)} %copy-done.2, f32[256,256]{1,0:T(8,128)S(1)} %copy-done, f32[256,256]{1,0:T(8,128)S(1)} %copy-done.1, f32[128,256]{1,0:T(8,128)S(1)} %copy-done.3, ...), custom_call_target="tpu_custom_call" | custom-call | bytes 1900544 | tf_op jit(solution)/shard_map/pallas_call | solution.py:225
  102.4 0.0 copy-start.7
  102.4 17.1 %all-to-all-start.3 = ((f32[128,4,128]{2,1,0:T(4,128)}), f32[128,4,128]{2,1,0:T(4,128)S(1)}, u32[]{:S(2)}, u32[]{:S(2)}) async-start(f32[128,4,128]{2,1,0:T(4,128)} %shard_map.159), calls=%async_computation.3 | async-start | bytes 524288 | tf_op jit(solution)/shard_map/all_to_all | solution.py:244
  119.5 0.0 copy-done.7
  119.5 0.0 copy-start.5
  119.5 0.0 copy-start.6
  119.5 0.8 shard_map.158
  120.3 1.9 %collective-permute-start = (f32[1,128]{1,0:T(1,128)S(1)}, f32[1,128]{1,0:T(1,128)S(1)}, u32[]{:S(2)}, u32[]{:S(2)}) collective-permute-start(f32[1,128]{1,0:T(1,128)S(1)} %get-tuple-element.29), channel_id=1, source_target_pairs={{0,4},{4,0},{8,12},{12,8},{16,20},{20,16},{24,28},{28,24},{32,36},... | collective-permute-start | bytes 1544 | tf_op jit(solution)/shard_map/ppermute | solution.py:296
  122.2 3.5 %collective-permute-done = f32[1,128]{1,0:T(1,128)S(1)} collective-permute-done((f32[1,128]{1,0:T(1,128)S(1)}, f32[1,128]{1,0:T(1,128)S(1)}, u32[]{:S(2)}, u32[]{:S(2)}) %collective-permute-start) | collective-permute-done | bytes 544 | tf_op jit(solution)/shard_map/ppermute | solution.py:296
  125.7 0.6 pad_maximum_fusion
  126.3 6.0 %all-to-all-done.3.got_ref = f32[128,4,128]{2,1,0:T(4,128)S(1)} async-done(((f32[128,4,128]{2,1,0:T(4,128)}), f32[128,4,128]{2,1,0:T(4,128)S(1)}, u32[]{:S(2)}, u32[]{:S(2)}) %all-to-all-start.3) | async-done | bytes 262176 | tf_op jit(solution)/shard_map/all_to_all | solution.py:244
  132.3 0.0 copy-done.5
  132.3 0.0 copy-done.6
  132.3 0.9 shard_map.160
  (1 shorter events, 0.0 us)
Async XLA Ops:
  0.6 39.1 %copy-start.2 = (f32[256,128]{1,0:T(8,128)S(1)}, f32[256,128]{1,0:T(8,128)}, u32[]{:S(2)}) copy-start(f32[256,128]{1,0:T(8,128)} %constant.18.clone.first_ref) | copy-start | bytes 393220
  0.6 39.1 %copy-start.3 = (f32[128,256]{1,0:T(8,128)S(1)}, f32[128,256]{1,0:T(8,128)}, u32[]{:S(2)}) copy-start(f32[128,256]{1,0:T(8,128)} %constant.21.clone.last_ref) | copy-start | bytes 393220
  0.7 39.1 %copy-start.4 = (f32[2,128,128]{2,1,0:T(8,128)S(1)}, f32[2,128,128]{2,1,0:T(8,128)}, u32[]{:S(2)}) copy-start(f32[2,128,128]{2,1,0:T(8,128)} %constant.22.clone.twist_ref) | copy-start | bytes 393220
  2.1 37.6 %copy-start = (f32[256,256]{1,0:T(8,128)S(1)}, f32[256,256]{1,0:T(8,128)}, u32[]{:S(2)}) copy-start(f32[256,256]{1,0:T(8,128)} %constant.19.clone.ahead_ref) | copy-start | bytes 786436
  2.1 37.6 %copy-start.1 = (f32[256,256]{1,0:T(8,128)S(1)}, f32[256,256]{1,0:T(8,128)}, u32[]{:S(2)}) copy-start(f32[256,256]{1,0:T(8,128)} %constant.20.clone.back_ref) | copy-start | bytes 786436
  102.4 17.1 %copy-start.7 = (f32[256]{0:T(256)S(1)}, f32[256]{0:T(256)}, u32[]{:S(2)}) copy-start(f32[256]{0:T(256)} %param.15) | copy-start | bytes 3076
  102.4 29.9 %all-to-all-start.3 = ((f32[128,4,128]{2,1,0:T(4,128)}), f32[128,4,128]{2,1,0:T(4,128)S(1)}, u32[]{:S(2)}, u32[]{:S(2)}) async-start(f32[128,4,128]{2,1,0:T(4,128)} %shard_map.159), calls=%async_computation.3 | async-start | bytes 524288 | tf_op jit(solution)/shard_map/all_to_all | solution.py:244
  119.5 12.8 %copy-start.5 = (bf16[128,256]{1,0:T(8,128)(2,1)S(1)}, bf16[128,256]{1,0:T(8,128)(2,1)}, u32[]{:S(2)}) copy-start(bf16[128,256]{1,0:T(8,128)(2,1)} %key_ref.1) | copy-start | bytes 196612
  119.5 12.8 %copy-start.6 = (bf16[128,256]{1,0:T(8,128)(2,1)S(1)}, bf16[128,256]{1,0:T(8,128)(2,1)}, u32[]{:S(2)}) copy-start(bf16[128,256]{1,0:T(8,128)(2,1)} %value_ref.1) | copy-start | bytes 196612
  120.3 5.4 %collective-permute-start = (f32[1,128]{1,0:T(1,128)S(1)}, f32[1,128]{1,0:T(1,128)S(1)}, u32[]{:S(2)}, u32[]{:S(2)}) collective-permute-start(f32[1,128]{1,0:T(1,128)S(1)} %get-tuple-element.29), channel_id=1, source_target_pairs={{0,4},{4,0},{8,12},{12,8},{16,20},{20,16},{24,28},{28,24},{32,36},... | collective-permute-start | bytes 1544 | tf_op jit(solution)/shard_map/ppermute | solution.py:296

commit v6 on v3

--- a/solution.py
+++ b/solution.py
@@ -38,27 +38,15 @@
     return tuple(t.astype(np.float32) for t in (first, ahead, back, last)) + (twist,)
 
 
-def halves(value):
-    high = value.astype(jnp.bfloat16)
-    low = (value - high.astype(jnp.float32)).astype(jnp.bfloat16)
-    return high, low
-
-
-def dot(left, right):
-    return jnp.dot(left, right, preferred_element_type=jnp.float32)
-
-
 def exact_dot(left, right):
-    (left_high, left_low), (right_high, right_low) = left, right
-    return dot(left_high, right_high) + (dot(left_high, right_low) + dot(left_low, right_high))
+    return jnp.dot(
+        left, right, precision=lax.Precision.HIGHEST, preferred_element_type=jnp.float32
+    )
 
 
 def forward_spectra(columns, first_ref, ahead_ref, twist_ref):
     count = len(columns)
-    high, low = halves(jnp.concatenate(columns, axis=1))
-    first_high, first_low = halves(first_ref[...])
-    mid = dot(jnp.concatenate([first_high, first_high], axis=1), jnp.concatenate([high, low], axis=0))
-    mid = mid + dot(first_low, high)
+    mid = exact_dot(first_ref[...], jnp.concatenate(columns, axis=1))
     cos_t, sin_t = twist_ref[0], twist_ref[1]
     rows = []
     for u in range(count):
@@ -67,7 +55,7 @@
         rows.append(
             jnp.concatenate([real * cos_t - imag * sin_t, real * sin_t + imag * cos_t], axis=1)
         )
-    out = exact_dot(halves(jnp.concatenate(rows, axis=0)), halves(ahead_ref[...]))
+    out = exact_dot(jnp.concatenate(rows, axis=0), ahead_ref[...])
     return [
         (out[u * side : (u + 1) * side, :side], out[u * side : (u + 1) * side, side:])
         for u in range(count)
@@ -77,7 +65,7 @@
 def inverse_columns(spectra, back_ref, last_ref, twist_ref):
     count = len(spectra)
     stacked = jnp.concatenate([jnp.concatenate(pair, axis=1) for pair in spectra], axis=0)
-    mid = exact_dot(halves(stacked), halves(back_ref[...]))
+    mid = exact_dot(stacked, back_ref[...])
     cos_t, sin_t = twist_ref[0], twist_ref[1]
     cols = []
     for u in range(count):
@@ -86,7 +74,7 @@
         cols.append(
             jnp.concatenate([real * cos_t + imag * sin_t, imag * cos_t - real * sin_t], axis=0)
         )
-    return exact_dot(halves(last_ref[...]), halves(jnp.concatenate(cols, axis=1)))
+    return exact_dot(last_ref[...], jnp.concatenate(cols, axis=1))
 
 
 def product(left, right):

time: 131 us -> 133 us (1.015)
  Pallas kernels: 6.51 us -> 8.45 us
    pallas_call x7, Pallas kernels: 6.51 us -> 8.45 us  [call(): pl.pallas_call(kernel, out_shape=outs, compiler_params=pltpu.CompilerPara...]
where the time goes in v6:
time: 133 us
  blocking collectives  94.2 us (71%)
  starting transfers between devices  19 us (14%)
  waiting for transfers between devices  9.5 us (7%)
  Pallas kernels  8.45 us (6%)
    all_to_all x3, blocking collectives, swap(): lax.all_to_all(sent.reshape(shape), 'ctx', split_axis=0, concat_axis=0, a...  89.2 us
    all_to_all x1, starting transfers between devices, swap(): lax.all_to_all(sent.reshape(shape), 'ctx', split_axis=0, concat_axis=0, a...  17.1 us
    pallas_call x7, Pallas kernels, call(): pl.pallas_call(kernel, out_shape=outs, compiler_params=pltpu.CompilerPara...  8.45 us
    all_to_all x1, waiting for transfers between devices, swap(): lax.all_to_all(sent.reshape(shape), 'ctx', split_axis=0, concat_axis=0, a...  5.99 us
    all_gather x1, blocking collectives, per_device(): sums = lax.all_gather(sums, 'tp')  5.07 us
    ppermute x1, waiting for transfers between devices, per_device(): lax.ppermute(gain_half, 'ctx', [(i, i ^ 1) for i in range(side)])  3.51 us
  transfers between devices with their start and end apart: 2, of which 2 were waited for; matrix products, arithmetic and copies ran while one was open for 0% of the time, Pallas kernels for 1%

profile of v6, /device:TPU:24, one launch (start us, length us, event | category | flops | bytes accessed | tf_op | source)
XLA Modules:
  0.0 132.6 jit_solution(4004136985459083168)
XLA Ops:
  0.6 0.0 copy-start.2
  0.6 0.0 copy-start.3
  0.7 0.0 copy-start.4
  0.7 1.4 %shard_map.154 = (f32[512,128]{1,0:T(8,128)S(1)}, f32[256,128]{1,0:T(8,128)S(1)}, f32[256,128]{1,0:T(8,128)S(1)}, f32[256,128]{1,0:T(8,128)S(1)}) custom-call(bf16[128,256]{1,0:T(8,128)(2,1)} %key_ref.1, bf16[128,256]{1,0:T(8,128)(2,1)} %value_ref.1, f32[128,256]{1,0:T(8,128)} %filt_hbm.1, bf16[128,256]{1,0:T(8,128)(2,1)} %query_hbm.1, ...), custom_call_target="tpu_custom_call" | custom-call | bytes 1049600 | tf_op jit(solution)/shard_map/pallas_call | solution.py:225
  2.0 0.0 copy-start
  2.0 0.0 copy-start.1
  2.1 37.6 %all_to_all.20 = f32[128,4,128]{2,1,0:T(4,128)S(1)} all-to-all(f32[128,4,128]{2,1,0:T(4,128)S(1)} %bitcast.19), channel_id=1, replica_groups={{392,136,396,140,384,128,388,132,408,152,412,156,400,144,404,148,424,16..., dimensions={0} | all-to-all | bytes 524288 | tf_op jit(solution)/shard_map/all_to_all | solution.py:245
  39.7 0.0 copy-done.2
  39.7 0.0 copy-done.3
  39.7 0.0 copy-done.4
  39.7 0.0 copy-done
  39.7 0.0 copy-done.1
  39.7 2.3 %shard_map.155 = (f32[256,128]{1,0:T(8,128)S(1)}, f32[4,2,128,128]{3,2,1,0:T(8,128)S(1)}) custom-call(f32[512,128]{1,0:T(8,128)S(1)} %bitcast.17, f32[256,128]{1,0:T(8,128)S(1)} %copy-done.2, f32[256,256]{1,0:T(8,128)S(1)} %copy-done, f32[256,256]{1,0:T(8,128)S(1)} %copy-done.1, f32[128,256]{1,0:T(8,128)S(1)} %copy-done.3, f32[2,128,128]{2,1,0:T(8,128)S(1)} %copy-done.4), custom_call_target="tpu_custom_call" | custom-call | bytes 1835008 | tf_op jit(solution)/shard_map/pallas_call | solution.py:225
  42.0 23.9 %all_to_all.21 = f32[128,2,128]{2,1,0:T(2,128)S(1)} all-to-all(f32[128,2,128]{2,1,0:T(2,128)S(1)} %bitcast.20), channel_id=1, replica_groups={{392,136,396,140,384,128,388,132,408,152,412,156,400,144,404,148,424,16..., dimensions={0} | all-to-all | bytes 262144 | tf_op jit(solution)/shard_map/all_to_all | solution.py:245
  65.9 5.1 %all-gather.1.sums_ref = f32[4,2,128]{2,1,0:T(2,128)S(1)} all-gather(f32[1,2,128]{2,1,0:T(2,128)S(1)} %bitcast.23), channel_id=2, replica_groups=mesh['ctx'=128,'tp'=4] {'tp'}, dimensions={0}, use_global_device_ids=true | all-gather | bytes 5120 | tf_op jit(solution)/shard_map/all_gather | solution.py:284
  71.0 0.2 shard_map.157
  71.2 27.6 %all_to_all.22 = f32[128,1,384]{2,1,0:T(1,128)S(1)} all-to-all(f32[128,1,384]{2,1,0:T(1,128)S(1)} %bitcast.18), channel_id=1, replica_groups={{392,136,396,140,384,128,388,132,408,152,412,156,400,144,404,148,424,16..., dimensions={0} | all-to-all | bytes 393216 | tf_op jit(solution)/shard_map/all_to_all | solution.py:245
  98.9 3.0 %shard_map.159 = f32[512,128]{1,0:T(8,128)} custom-call(f32[384,128]{1,0:T(8,128)S(1)} %bitcast.14, f32[4,2,128,128]{3,2,1,0:T(8,128)S(1)} %get-tuple-element.25.spec_ref, f32[256,128]{1,0:T(8,128)S(1)} %copy-done.2, f32[256,256]{1,0:T(8,128)S(1)} %copy-done, f32[256,256]{1,0:T(8,128)S(1)} %copy-done.1, f32[128,256]{1,0:T(8,128)S(1)} %copy-done.3, ...), custom_call_target="tpu_custom_call" | custom-call | bytes 1900544 | tf_op jit(solution)/shard_map/pallas_call | solution.py:225
  101.8 0.0 copy-start.7
  101.8 17.1 %all-to-all-start.3 = ((f32[128,4,128]{2,1,0:T(4,128)}), f32[128,4,128]{2,1,0:T(4,128)S(1)}, u32[]{:S(2)}, u32[]{:S(2)}) async-start(f32[128,4,128]{2,1,0:T(4,128)} %bitcast.8), calls=%async_computation.3 | async-start | bytes 524288 | tf_op jit(solution)/shard_map/all_to_all | solution.py:245
  118.9 0.0 copy-done.7
  118.9 0.0 copy-start.5
  118.9 0.0 copy-start.6
  118.9 0.8 shard_map.158
  119.7 1.9 %collective-permute-start = (f32[1,128]{1,0:T(1,128)S(1)}, f32[1,128]{1,0:T(1,128)S(1)}, u32[]{:S(2)}, u32[]{:S(2)}) collective-permute-start(f32[1,128]{1,0:T(1,128)S(1)} %get-tuple-element.29), channel_id=1, source_target_pairs={{0,4},{4,0},{8,12},{12,8},{16,20},{20,16},{24,28},{28,24},{32,36},... | collective-permute-start | bytes 1544 | tf_op jit(solution)/shard_map/ppermute | solution.py:297
  121.6 3.5 %collective-permute-done = f32[1,128]{1,0:T(1,128)S(1)} collective-permute-done((f32[1,128]{1,0:T(1,128)S(1)}, f32[1,128]{1,0:T(1,128)S(1)}, u32[]{:S(2)}, u32[]{:S(2)}) %collective-permute-start) | collective-permute-done | bytes 544 | tf_op jit(solution)/shard_map/ppermute | solution.py:297
  125.2 0.6 pad_maximum_fusion
  125.7 6.0 %all-to-all-done.3 = f32[128,4,128]{2,1,0:T(4,128)S(1)} async-done(((f32[128,4,128]{2,1,0:T(4,128)}), f32[128,4,128]{2,1,0:T(4,128)S(1)}, u32[]{:S(2)}, u32[]{:S(2)}) %all-to-all-start.3) | async-done | bytes 262176 | tf_op jit(solution)/shard_map/all_to_all | solution.py:245
  131.7 0.0 copy-done.5
  131.7 0.0 copy-done.6
  131.7 0.8 shard_map.160
  (2 shorter events, 0.0 us)
Async XLA Ops:
  0.6 39.0 %copy-start.2 = (f32[256,128]{1,0:T(8,128)S(1)}, f32[256,128]{1,0:T(8,128)}, u32[]{:S(2)}) copy-start(f32[256,128]{1,0:T(8,128)} %constant.18.clone.first_ref) | copy-start | bytes 393220
  0.6 39.0 %copy-start.3 = (f32[128,256]{1,0:T(8,128)S(1)}, f32[128,256]{1,0:T(8,128)}, u32[]{:S(2)}) copy-start(f32[128,256]{1,0:T(8,128)} %constant.21.clone.last_ref) | copy-start | bytes 393220
  0.7 39.0 %copy-start.4 = (f32[2,128,128]{2,1,0:T(8,128)S(1)}, f32[2,128,128]{2,1,0:T(8,128)}, u32[]{:S(2)}) copy-start(f32[2,128,128]{2,1,0:T(8,128)} %constant.22.clone.twist_ref) | copy-start | bytes 393220
  2.0 37.6 %copy-start = (f32[256,256]{1,0:T(8,128)S(1)}, f32[256,256]{1,0:T(8,128)}, u32[]{:S(2)}) copy-start(f32[256,256]{1,0:T(8,128)} %constant.19.clone.ahead_ref) | copy-start | bytes 786436
  2.0 37.6 %copy-start.1 = (f32[256,256]{1,0:T(8,128)S(1)}, f32[256,256]{1,0:T(8,128)}, u32[]{:S(2)}) copy-start(f32[256,256]{1,0:T(8,128)} %constant.20.clone.back_ref) | copy-start | bytes 786436
  101.8 17.1 %copy-start.7 = (f32[256]{0:T(256)S(1)}, f32[256]{0:T(256)}, u32[]{:S(2)}) copy-start(f32[256]{0:T(256)} %param.15) | copy-start | bytes 3076
  101.8 29.9 %all-to-all-start.3 = ((f32[128,4,128]{2,1,0:T(4,128)}), f32[128,4,128]{2,1,0:T(4,128)S(1)}, u32[]{:S(2)}, u32[]{:S(2)}) async-start(f32[128,4,128]{2,1,0:T(4,128)} %bitcast.8), calls=%async_computation.3 | async-start | bytes 524288 | tf_op jit(solution)/shard_map/all_to_all | solution.py:245
  118.9 12.8 %copy-start.5 = (bf16[128,256]{1,0:T(8,128)(2,1)S(1)}, bf16[128,256]{1,0:T(8,128)(2,1)}, u32[]{:S(2)}) copy-start(bf16[128,256]{1,0:T(8,128)(2,1)} %key_ref.1) | copy-start | bytes 196612
  118.9 12.8 %copy-start.6 = (bf16[128,256]{1,0:T(8,128)(2,1)S(1)}, bf16[128,256]{1,0:T(8,128)(2,1)}, u32[]{:S(2)}) copy-start(bf16[128,256]{1,0:T(8,128)(2,1)} %value_ref.1) | copy-start | bytes 196612
  119.7 5.4 %collective-permute-start = (f32[1,128]{1,0:T(1,128)S(1)}, f32[1,128]{1,0:T(1,128)S(1)}, u32[]{:S(2)}, u32[]{:S(2)}) collective-permute-start(f32[1,128]{1,0:T(1,128)S(1)} %get-tuple-element.29), channel_id=1, source_target_pairs={{0,4},{4,0},{8,12},{12,8},{16,20},{20,16},{24,28},{28,24},{32,36},... | collective-permute-start | bytes 1544 | tf_op jit(solution)/shard_map/ppermute | solution.py:297

commit v7 on v3

--- a/solution.py
+++ b/solution.py
@@ -102,8 +102,8 @@
 
 
 def first_kernel(key_hbm, value_hbm, filt_hbm, query_hbm, cot_hbm, gain_hbm, *refs):
-    sent_ref, query_t_ref, cot_t_ref, scaled_t_ref = refs[:4]
-    key_ref, value_ref, filt_ref, query_ref, cot_ref, gain_ref, sems = refs[4:]
+    sent_ref, query_t_ref, scaled_t_ref = refs[:3]
+    key_ref, value_ref, filt_ref, query_ref, cot_ref, gain_ref, sems = refs[3:]
     sources = (filt_hbm, key_hbm, value_hbm, query_hbm, cot_hbm, gain_hbm)
     targets = (filt_ref, key_ref, value_ref, query_ref, cot_ref, gain_ref)
     copies = [
@@ -124,8 +124,7 @@
         copy.wait()
     for h, cols in enumerate(halves_of):
         cot = cot_ref[:, cols].astype(jnp.float32)
-        query_t_ref[cols, :] = query_ref[:, cols].astype(jnp.float32).T
-        cot_t_ref[cols, :] = cot.T
+        query_t_ref[cols, :] = query_ref[:, cols].T.astype(jnp.float32)
         scaled_t_ref[cols, :] = (cot * gain_ref[:, cols]).T
 
 
@@ -163,18 +162,17 @@
     return inv_rms, dots * (1.0 / channels)
 
 
-def d_conv_kernel(conv_ref, query_t_ref, cot_t_ref, scaled_t_ref, sums_ref, out_ref):
+def d_conv_kernel(conv_ref, query_t_ref, scaled_t_ref, sums_ref, out_ref):
     inv_rms, row_dot = row_scalars(sums_ref)
     pull = inv_rms * inv_rms * inv_rms * row_dot
     parts = []
     for h in range(2):
         cols = slice(h * side, (h + 1) * side)
         query = query_t_ref[cols, :]
-        cot = cot_t_ref[cols, :]
         gated = conv_ref[every(h, 2), :] * query
         scaled = scaled_t_ref[cols, :]
         out_ref[every(h, 3), :] = (inv_rms * scaled - gated * pull) * query
-        part = jnp.sum(cot * gated * inv_rms, axis=1, keepdims=True)
+        part = jnp.sum(scaled * gated * inv_rms, axis=1, keepdims=True)
         parts.append(jnp.broadcast_to(part, (side, side)).T)
     number = lax.broadcasted_iota(jnp.int32, (side, side), 0)
     out_ref[every(2, 3), :] = jnp.where((number & 2) == 0, parts[0], parts[1])
@@ -272,9 +270,9 @@
 
     in_hbm = pl.BlockSpec(memory_space=pltpu.HBM)
     inputs = (key_proj, value_proj, long_filter, gate_query, cotangent, gain)
-    sent, query_t, cot_t, scaled_t = call(
+    sent, query_t, scaled_t = call(
         first_kernel,
-        (f32(4 * side, side),) + (f32(wide, side),) * 3,
+        (f32(4 * side, side),) + (f32(wide, side),) * 2,
         *(pltpu.with_memory_space_constraint(x, pltpu.HBM) for x in inputs),
         in_specs=[in_hbm] * 6,
         scratch_shapes=[
@@ -294,7 +292,7 @@
     conv_t = swap(sent, 2)
     (sums,) = call(row_sums_kernel, (f32(2, side),), conv_t, query_t, scaled_t)
     sums = lax.all_gather(sums, "tp")
-    (sent,) = call(d_conv_kernel, (f32(3 * side, side),), conv_t, query_t, cot_t, scaled_t, sums)
+    (sent,) = call(d_conv_kernel, (f32(3 * side, side),), conv_t, query_t, scaled_t, sums)
     got = swap(sent, 3)
     output, grad_query, gain_half = call(
         row_outputs_kernel,
@@ -327,7 +325,8 @@
         key_proj,
         value_proj,
     )
-    return (output, grad_query, grad_key, grad_value, grad_filter, grad_gain.reshape(wide))
+    grad_gain = (grad_gain / gain).reshape(wide)
+    return (output, grad_query, grad_key, grad_value, grad_filter, grad_gain)
 
 
 def solution(mesh):

time: 131 us -> 131 us (level)
  no operation moved by 1% of the time
where the time goes in v7:
time: 131 us
  blocking collectives  94.2 us (72%)
  starting transfers between devices  19 us (15%)
  waiting for transfers between devices  9.5 us (7%)
  Pallas kernels  6.49 us (5%)
    all_to_all x3, blocking collectives, swap(): lax.all_to_all(sent.reshape(shape), 'ctx', split_axis=0, concat_axis=0, a...  89.2 us
    all_to_all x1, starting transfers between devices, swap(): lax.all_to_all(sent.reshape(shape), 'ctx', split_axis=0, concat_axis=0, a...  17.1 us
    pallas_call x7, Pallas kernels, call(): pl.pallas_call(kernel, out_shape=outs, compiler_params=pltpu.CompilerPara...  6.49 us
    all_to_all x1, waiting for transfers between devices, swap(): lax.all_to_all(sent.reshape(shape), 'ctx', split_axis=0, concat_axis=0, a...  5.99 us
    all_gather x1, blocking collectives, per_device(): sums = lax.all_gather(sums, 'tp')  5.07 us
    ppermute x1, waiting for transfers between devices, per_device(): lax.ppermute(gain_half, 'ctx', [(i, i ^ 1) for i in range(side)])  3.51 us
  transfers between devices with their start and end apart: 2, of which 2 were waited for; matrix products, arithmetic and copies ran while one was open for 0% of the time, Pallas kernels for 1%

profile of v7, /device:TPU:24, one launch (start us, length us, event | category | flops | bytes accessed | tf_op | source)
XLA Modules:
  0.0 130.6 jit_solution(7306147408915917376)
XLA Ops:
  0.6 0.0 copy-start.2
  0.6 0.0 copy-start.3
  0.7 0.0 copy-start.4
  0.7 1.3 %shard_map.154 = (f32[512,128]{1,0:T(8,128)S(1)}, f32[256,128]{1,0:T(8,128)S(1)}, f32[256,128]{1,0:T(8,128)S(1)}) custom-call(bf16[128,256]{1,0:T(8,128)(2,1)} %key_ref.1, bf16[128,256]{1,0:T(8,128)(2,1)} %value_ref.1, f32[128,256]{1,0:T(8,128)} %filt_hbm.1, bf16[128,256]{1,0:T(8,128)(2,1)} %query_hbm.1, bf16[128,256]{1,0:T(8,128)(2,1)} %cot_hbm.1, ...), custom_call_target="tpu_custom_call" | custom-call | bytes 918528 | tf_op jit(solution)/shard_map/pallas_call | solution.py:235
  2.0 0.0 copy-start
  2.0 0.0 copy-start.1
  2.0 37.6 %all_to_all.20 = f32[128,4,128]{2,1,0:T(4,128)S(1)} all-to-all(f32[128,4,128]{2,1,0:T(4,128)S(1)} %bitcast.22), channel_id=1, replica_groups={{392,136,396,140,384,128,388,132,408,152,412,156,400,144,404,148,424,16..., dimensions={0} | all-to-all | bytes 524288 | tf_op jit(solution)/shard_map/all_to_all | solution.py:255
  39.7 0.0 copy-done.2
  39.7 0.0 copy-done.3
  39.7 0.0 copy-done.4
  39.7 0.0 copy-done
  39.7 0.0 copy-done.1
  39.7 1.3 shard_map.155
  41.0 23.9 %all_to_all.21 = f32[128,2,128]{2,1,0:T(2,128)S(1)} all-to-all(f32[128,2,128]{2,1,0:T(2,128)S(1)} %bitcast.23), channel_id=1, replica_groups={{392,136,396,140,384,128,388,132,408,152,412,156,400,144,404,148,424,16..., dimensions={0} | all-to-all | bytes 262144 | tf_op jit(solution)/shard_map/all_to_all | solution.py:255
  64.9 5.1 %all-gather.1.sums_ref = f32[4,2,128]{2,1,0:T(2,128)S(1)} all-gather(f32[1,2,128]{2,1,0:T(2,128)S(1)} %bitcast.26), channel_id=2, replica_groups=mesh['ctx'=128,'tp'=4] {'tp'}, dimensions={0}, use_global_device_ids=true | all-gather | bytes 5120 | tf_op jit(solution)/shard_map/all_gather | solution.py:294
  70.0 0.2 shard_map.157
  70.2 27.6 %all_to_all.22 = f32[128,1,384]{2,1,0:T(1,128)S(1)} all-to-all(f32[128,1,384]{2,1,0:T(1,128)S(1)} %bitcast.21), channel_id=1, replica_groups={{392,136,396,140,384,128,388,132,408,152,412,156,400,144,404,148,424,16..., dimensions={0} | all-to-all | bytes 393216 | tf_op jit(solution)/shard_map/all_to_all | solution.py:255
  97.8 2.0 %shard_map.159 = f32[512,128]{1,0:T(8,128)} custom-call(f32[384,128]{1,0:T(8,128)S(1)} %bitcast.17, f32[4,2,128,128]{3,2,1,0:T(8,128)S(1)} %get-tuple-element.23.spec_ref, f32[256,128]{1,0:T(8,128)S(1)} %copy-done.2, f32[256,256]{1,0:T(8,128)S(1)} %copy-done, f32[256,256]{1,0:T(8,128)S(1)} %copy-done.1, f32[128,256]{1,0:T(8,128)S(1)} %copy-done.3, ...), custom_call_target="tpu_custom_call" | custom-call | bytes 1900544 | tf_op jit(solution)/shard_map/pallas_call | solution.py:235
  99.9 0.0 copy-start.7
  99.9 17.1 %all-to-all-start.3 = ((f32[128,4,128]{2,1,0:T(4,128)}), f32[128,4,128]{2,1,0:T(4,128)S(1)}, u32[]{:S(2)}, u32[]{:S(2)}) async-start(f32[128,4,128]{2,1,0:T(4,128)} %bitcast.8), calls=%async_computation.3 | async-start | bytes 524288 | tf_op jit(solution)/shard_map/all_to_all | solution.py:255
  116.9 0.0 copy-done.7
  117.0 0.0 copy-start.5
  117.0 0.0 copy-start.6
  117.0 0.8 shard_map.158
  117.8 1.9 %collective-permute-start = (f32[1,128]{1,0:T(1,128)S(1)}, f32[1,128]{1,0:T(1,128)S(1)}, u32[]{:S(2)}, u32[]{:S(2)}) collective-permute-start(f32[1,128]{1,0:T(1,128)S(1)} %get-tuple-element.27), channel_id=1, source_target_pairs={{0,4},{4,0},{8,12},{12,8},{16,20},{20,16},{24,28},{28,24},{32,36},... | collective-permute-start | bytes 1544 | tf_op jit(solution)/shard_map/ppermute | solution.py:307
  119.7 3.5 %collective-permute-done = f32[1,128]{1,0:T(1,128)S(1)} collective-permute-done((f32[1,128]{1,0:T(1,128)S(1)}, f32[1,128]{1,0:T(1,128)S(1)}, u32[]{:S(2)}, u32[]{:S(2)}) %collective-permute-start) | collective-permute-done | bytes 544 | tf_op jit(solution)/shard_map/ppermute | solution.py:307
  123.2 0.6 maximum_divide_fusion
  123.8 6.0 %all-to-all-done.3 = f32[128,4,128]{2,1,0:T(4,128)S(1)} async-done(((f32[128,4,128]{2,1,0:T(4,128)}), f32[128,4,128]{2,1,0:T(4,128)S(1)}, u32[]{:S(2)}, u32[]{:S(2)}) %all-to-all-start.3) | async-done | bytes 262176 | tf_op jit(solution)/shard_map/all_to_all | solution.py:255
  129.8 0.0 copy-done.5
  129.8 0.0 copy-done.6
  129.8 0.8 shard_map.160
  (2 shorter events, 0.0 us)
Async XLA Ops:
  0.6 39.0 %copy-start.2 = (f32[256,128]{1,0:T(8,128)S(1)}, f32[256,128]{1,0:T(8,128)}, u32[]{:S(2)}) copy-start(f32[256,128]{1,0:T(8,128)} %constant.18.clone.first_ref) | copy-start | bytes 393220
  0.6 39.0 %copy-start.3 = (f32[128,256]{1,0:T(8,128)S(1)}, f32[128,256]{1,0:T(8,128)}, u32[]{:S(2)}) copy-start(f32[128,256]{1,0:T(8,128)} %constant.21.clone.last_ref) | copy-start | bytes 393220
  0.7 39.0 %copy-start.4 = (f32[2,128,128]{2,1,0:T(8,128)S(1)}, f32[2,128,128]{2,1,0:T(8,128)}, u32[]{:S(2)}) copy-start(f32[2,128,128]{2,1,0:T(8,128)} %constant.22.clone.twist_ref) | copy-start | bytes 393220
  2.0 37.6 %copy-start = (f32[256,256]{1,0:T(8,128)S(1)}, f32[256,256]{1,0:T(8,128)}, u32[]{:S(2)}) copy-start(f32[256,256]{1,0:T(8,128)} %constant.19.clone.ahead_ref) | copy-start | bytes 786436
  2.0 37.6 %copy-start.1 = (f32[256,256]{1,0:T(8,128)S(1)}, f32[256,256]{1,0:T(8,128)}, u32[]{:S(2)}) copy-start(f32[256,256]{1,0:T(8,128)} %constant.20.clone.back_ref) | copy-start | bytes 786436
  99.9 17.1 %copy-start.7 = (f32[256]{0:T(256)S(1)}, f32[256]{0:T(256)}, u32[]{:S(2)}) copy-start(f32[256]{0:T(256)} %param.15) | copy-start | bytes 3076
  99.9 29.9 %all-to-all-start.3 = ((f32[128,4,128]{2,1,0:T(4,128)}), f32[128,4,128]{2,1,0:T(4,128)S(1)}, u32[]{:S(2)}, u32[]{:S(2)}) async-start(f32[128,4,128]{2,1,0:T(4,128)} %bitcast.8), calls=%async_computation.3 | async-start | bytes 524288 | tf_op jit(solution)/shard_map/all_to_all | solution.py:255
  117.0 12.8 %copy-start.5 = (bf16[128,256]{1,0:T(8,128)(2,1)S(1)}, bf16[128,256]{1,0:T(8,128)(2,1)}, u32[]{:S(2)}) copy-start(bf16[128,256]{1,0:T(8,128)(2,1)} %key_ref.1) | copy-start | bytes 196612
  117.0 12.8 %copy-start.6 = (bf16[128,256]{1,0:T(8,128)(2,1)S(1)}, bf16[128,256]{1,0:T(8,128)(2,1)}, u32[]{:S(2)}) copy-start(bf16[128,256]{1,0:T(8,128)(2,1)} %value_ref.1) | copy-start | bytes 196612
  117.8 5.4 %collective-permute-start = (f32[1,128]{1,0:T(1,128)S(1)}, f32[1,128]{1,0:T(1,128)S(1)}, u32[]{:S(2)}, u32[]{:S(2)}) collective-permute-start(f32[1,128]{1,0:T(1,128)S(1)} %get-tuple-element.27), channel_id=1, source_target_pairs={{0,4},{4,0},{8,12},{12,8},{16,20},{20,16},{24,28},{28,24},{32,36},... | collective-permute-start | bytes 1544 | tf_op jit(solution)/shard_map/ppermute | solution.py:307

commit v8 on v7

--- a/solution.py
+++ b/solution.py
@@ -18,7 +18,8 @@
 
 def swap_order():
     grid = np.arange(side).reshape(ctx_sizes).transpose(1, 2, 0)
-    return np.roll(grid, (8, 2, 1), axis=(0, 1, 2)).reshape(-1).tolist()
+    grid = np.roll(grid, (7, 2, 1), axis=(0, 1, 2))
+    return grid[[0] + list(range(15, 0, -1))].reshape(-1).tolist()
 
 
 def make_tables():

time: 131 us -> 131 us (level)
  no operation moved by 1% of the time
where the time goes in v8:
time: 131 us
  blocking collectives  94.2 us (72%)
  starting transfers between devices  18.4 us (14%)
  waiting for transfers between devices  10.1 us (8%)
  Pallas kernels  6.49 us (5%)
    all_to_all x3, blocking collectives, swap(): lax.all_to_all(sent.reshape(shape), 'ctx', split_axis=0, concat_axis=0, a...  89.1 us
    all_to_all x1, starting transfers between devices, swap(): lax.all_to_all(sent.reshape(shape), 'ctx', split_axis=0, concat_axis=0, a...  16.4 us
    all_to_all x1, waiting for transfers between devices, swap(): lax.all_to_all(sent.reshape(shape), 'ctx', split_axis=0, concat_axis=0, a...  6.64 us
    pallas_call x7, Pallas kernels, call(): pl.pallas_call(kernel, out_shape=outs, compiler_params=pltpu.CompilerPara...  6.49 us
    all_gather x1, blocking collectives, per_device(): sums = lax.all_gather(sums, 'tp')  5.07 us
    ppermute x1, waiting for transfers between devices, per_device(): lax.ppermute(gain_half, 'ctx', [(i, i ^ 1) for i in range(side)])  3.51 us
  transfers between devices with their start and end apart: 2, of which 2 were waited for; matrix products, arithmetic and copies ran while one was open for 0% of the time, Pallas kernels for 1%

profile of v8, /device:TPU:24, one launch (start us, length us, event | category | flops | bytes accessed | tf_op | source)
XLA Modules:
  0.0 130.5 jit_solution(6062475198863911794)
XLA Ops:
  0.6 0.0 copy-start.2
  0.6 0.0 copy-start.3
  0.7 0.0 copy-start.4
  0.7 1.3 %shard_map.154 = (f32[512,128]{1,0:T(8,128)S(1)}, f32[256,128]{1,0:T(8,128)S(1)}, f32[256,128]{1,0:T(8,128)S(1)}) custom-call(bf16[128,256]{1,0:T(8,128)(2,1)} %key_ref.1, bf16[128,256]{1,0:T(8,128)(2,1)} %value_ref.1, f32[128,256]{1,0:T(8,128)} %filt_hbm.1, bf16[128,256]{1,0:T(8,128)(2,1)} %query_hbm.1, bf16[128,256]{1,0:T(8,128)(2,1)} %cot_hbm.1, ...), custom_call_target="tpu_custom_call" | custom-call | bytes 918528 | tf_op jit(solution)/shard_map/pallas_call | solution.py:236
  2.0 0.0 copy-start
  2.0 0.0 copy-start.1
  2.0 37.5 %all_to_all.20 = f32[128,4,128]{2,1,0:T(4,128)S(1)} all-to-all(f32[128,4,128]{2,1,0:T(4,128)S(1)} %bitcast.22), channel_id=1, replica_groups={{408,152,412,156,400,144,404,148,392,136,396,140,384,128,388,132,376,12..., dimensions={0} | all-to-all | bytes 524288 | tf_op jit(solution)/shard_map/all_to_all | solution.py:256
  39.5 0.0 copy-done.2
  39.5 0.0 copy-done.3
  39.5 0.0 copy-done.4
  39.5 0.0 copy-done
  39.5 0.0 copy-done.1
  39.5 1.3 shard_map.155
  40.8 23.7 %all_to_all.21 = f32[128,2,128]{2,1,0:T(2,128)S(1)} all-to-all(f32[128,2,128]{2,1,0:T(2,128)S(1)} %bitcast.23), channel_id=1, replica_groups={{408,152,412,156,400,144,404,148,392,136,396,140,384,128,388,132,376,12..., dimensions={0} | all-to-all | bytes 262144 | tf_op jit(solution)/shard_map/all_to_all | solution.py:256
  64.6 5.1 %all-gather.1.sums_ref = f32[4,2,128]{2,1,0:T(2,128)S(1)} all-gather(f32[1,2,128]{2,1,0:T(2,128)S(1)} %bitcast.26), channel_id=2, replica_groups=mesh['ctx'=128,'tp'=4] {'tp'}, dimensions={0}, use_global_device_ids=true | all-gather | bytes 5120 | tf_op jit(solution)/shard_map/all_gather | solution.py:295
  69.6 0.2 shard_map.157
  69.8 27.9 %all_to_all.22 = f32[128,1,384]{2,1,0:T(1,128)S(1)} all-to-all(f32[128,1,384]{2,1,0:T(1,128)S(1)} %bitcast.21), channel_id=1, replica_groups={{408,152,412,156,400,144,404,148,392,136,396,140,384,128,388,132,376,12..., dimensions={0} | all-to-all | bytes 393216 | tf_op jit(solution)/shard_map/all_to_all | solution.py:256
  97.8 2.0 %shard_map.159 = f32[512,128]{1,0:T(8,128)} custom-call(f32[384,128]{1,0:T(8,128)S(1)} %bitcast.17, f32[4,2,128,128]{3,2,1,0:T(8,128)S(1)} %get-tuple-element.23.spec_ref, f32[256,128]{1,0:T(8,128)S(1)} %copy-done.2, f32[256,256]{1,0:T(8,128)S(1)} %copy-done, f32[256,256]{1,0:T(8,128)S(1)} %copy-done.1, f32[128,256]{1,0:T(8,128)S(1)} %copy-done.3, ...), custom_call_target="tpu_custom_call" | custom-call | bytes 1900544 | tf_op jit(solution)/shard_map/pallas_call | solution.py:236
  99.8 0.0 copy-start.7
  99.8 16.4 %all-to-all-start.3 = ((f32[128,4,128]{2,1,0:T(4,128)}), f32[128,4,128]{2,1,0:T(4,128)S(1)}, u32[]{:S(2)}, u32[]{:S(2)}) async-start(f32[128,4,128]{2,1,0:T(4,128)} %bitcast.8), calls=%async_computation.3 | async-start | bytes 524288 | tf_op jit(solution)/shard_map/all_to_all | solution.py:256
  116.2 0.0 copy-done.7
  116.3 0.0 copy-start.5
  116.3 0.0 copy-start.6
  116.3 0.8 shard_map.158
  117.1 1.9 %collective-permute-start = (f32[1,128]{1,0:T(1,128)S(1)}, f32[1,128]{1,0:T(1,128)S(1)}, u32[]{:S(2)}, u32[]{:S(2)}) collective-permute-start(f32[1,128]{1,0:T(1,128)S(1)} %get-tuple-element.27), channel_id=1, source_target_pairs={{0,4},{4,0},{8,12},{12,8},{16,20},{20,16},{24,28},{28,24},{32,36},... | collective-permute-start | bytes 1544 | tf_op jit(solution)/shard_map/ppermute | solution.py:308
  119.0 3.5 %collective-permute-done = f32[1,128]{1,0:T(1,128)S(1)} collective-permute-done((f32[1,128]{1,0:T(1,128)S(1)}, f32[1,128]{1,0:T(1,128)S(1)}, u32[]{:S(2)}, u32[]{:S(2)}) %collective-permute-start) | collective-permute-done | bytes 544 | tf_op jit(solution)/shard_map/ppermute | solution.py:308
  122.5 0.6 maximum_divide_fusion
  123.1 6.6 %all-to-all-done.3 = f32[128,4,128]{2,1,0:T(4,128)S(1)} async-done(((f32[128,4,128]{2,1,0:T(4,128)}), f32[128,4,128]{2,1,0:T(4,128)S(1)}, u32[]{:S(2)}, u32[]{:S(2)}) %all-to-all-start.3) | async-done | bytes 262176 | tf_op jit(solution)/shard_map/all_to_all | solution.py:256
  129.7 0.0 copy-done.5
  129.7 0.0 copy-done.6
  129.7 0.8 shard_map.160
  (2 shorter events, 0.0 us)
Async XLA Ops:
  0.6 38.9 %copy-start.2 = (f32[256,128]{1,0:T(8,128)S(1)}, f32[256,128]{1,0:T(8,128)}, u32[]{:S(2)}) copy-start(f32[256,128]{1,0:T(8,128)} %constant.18.clone.first_ref) | copy-start | bytes 393220
  0.6 38.9 %copy-start.3 = (f32[128,256]{1,0:T(8,128)S(1)}, f32[128,256]{1,0:T(8,128)}, u32[]{:S(2)}) copy-start(f32[128,256]{1,0:T(8,128)} %constant.21.clone.last_ref) | copy-start | bytes 393220
  0.7 38.9 %copy-start.4 = (f32[2,128,128]{2,1,0:T(8,128)S(1)}, f32[2,128,128]{2,1,0:T(8,128)}, u32[]{:S(2)}) copy-start(f32[2,128,128]{2,1,0:T(8,128)} %constant.22.clone.twist_ref) | copy-start | bytes 393220
  2.0 37.5 %copy-start = (f32[256,256]{1,0:T(8,128)S(1)}, f32[256,256]{1,0:T(8,128)}, u32[]{:S(2)}) copy-start(f32[256,256]{1,0:T(8,128)} %constant.19.clone.ahead_ref) | copy-start | bytes 786436
  2.0 37.5 %copy-start.1 = (f32[256,256]{1,0:T(8,128)S(1)}, f32[256,256]{1,0:T(8,128)}, u32[]{:S(2)}) copy-start(f32[256,256]{1,0:T(8,128)} %constant.20.clone.back_ref) | copy-start | bytes 786436
  99.8 16.5 %copy-start.7 = (f32[256]{0:T(256)S(1)}, f32[256]{0:T(256)}, u32[]{:S(2)}) copy-start(f32[256]{0:T(256)} %param.15) | copy-start | bytes 3076
  99.8 29.9 %all-to-all-start.3 = ((f32[128,4,128]{2,1,0:T(4,128)}), f32[128,4,128]{2,1,0:T(4,128)S(1)}, u32[]{:S(2)}, u32[]{:S(2)}) async-start(f32[128,4,128]{2,1,0:T(4,128)} %bitcast.8), calls=%async_computation.3 | async-start | bytes 524288 | tf_op jit(solution)/shard_map/all_to_all | solution.py:256
  116.3 13.5 %copy-start.5 = (bf16[128,256]{1,0:T(8,128)(2,1)S(1)}, bf16[128,256]{1,0:T(8,128)(2,1)}, u32[]{:S(2)}) copy-start(bf16[128,256]{1,0:T(8,128)(2,1)} %key_ref.1) | copy-start | bytes 196612
  116.3 13.4 %copy-start.6 = (bf16[128,256]{1,0:T(8,128)(2,1)S(1)}, bf16[128,256]{1,0:T(8,128)(2,1)}, u32[]{:S(2)}) copy-start(bf16[128,256]{1,0:T(8,128)(2,1)} %value_ref.1) | copy-start | bytes 196612
  117.1 5.4 %collective-permute-start = (f32[1,128]{1,0:T(1,128)S(1)}, f32[1,128]{1,0:T(1,128)S(1)}, u32[]{:S(2)}, u32[]{:S(2)}) collective-permute-start(f32[1,128]{1,0:T(1,128)S(1)} %get-tuple-element.27), channel_id=1, source_target_pairs={{0,4},{4,0},{8,12},{12,8},{16,20},{20,16},{24,28},{28,24},{32,36},... | collective-permute-start | bytes 1544 | tf_op jit(solution)/shard_map/ppermute | solution.py:308
